TPU v7x, 512 devices: a whole 4x8x8 slice. The times are simulated.
512 devices in a mesh: row: 32 (over z, y_lo), col: 16 (over y_hi, x, core).
Axes of the slice: x: 4, y: 8 (y_hi: 2, y_lo: 4; y = y_hi * 4 + y_lo), z: 8, core: 2. Of those that a mesh axis runs over, the one named last changes fastest.
Arguments:
- pair: bfloat16 [448, 448, 128], P('row', 'col'), may hold values from -6 to 6
- out_norm_gain: float32 [128], replicated, may hold values from 0.1 to 1.9
- out_norm_bias: float32 [128], replicated, may hold values from -3 to 3
- out_weight_in: bfloat16 [128, 640], replicated, may hold values from -0.5 to 0.5
- out_mix_gain: float32 [128], replicated, may hold values from 0.1 to 1.9
- out_mix_bias: float32 [128], replicated, may hold values from -3 to 3
- out_weight_out: bfloat16 [128, 128], replicated, may hold values from -0.5 to 0.5
- in_norm_gain: float32 [128], replicated, may hold values from 0.1 to 1.9
- in_norm_bias: float32 [128], replicated, may hold values from -3 to 3
- in_weight_in: bfloat16 [128, 640], replicated, may hold values from -0.5 to 0.5
- in_mix_gain: float32 [128], replicated, may hold values from 0.1 to 1.9
- in_mix_bias: float32 [128], replicated, may hold values from -3 to 3
- in_weight_out: bfloat16 [128, 128], replicated, may hold values from -0.5 to 0.5
Outputs:
- updated: bfloat16 [448, 448, 128], P('row', 'col')
All inputs are finite; a program needn't handle non-finite values.
Results may differ from a plain program's by a relative error of at most 0.013.
Values may be sent and summed in bfloat16 or wider, within the bound.
No kernel may reach another device: no remote copies, remote signals or barrier semaphores. Data moves between devices by JAX's collectives and lax.ppermute only.
A program may use at most 64 MiB of HBM per device.

v0:
```python
import jax
import jax.numpy as jnp
from jax import lax
from jax.sharding import PartitionSpec as P

CH = 128


EPSILON = 1e-05


def spread_2(value, axis, source):
    kept = jnp.where(lax.axis_index(axis) == source, value, 0).astype(value.dtype)
    return lax.psum(kept, axis)


def layer_norm(values, gain, bias):
    center = values - jnp.mean(values, axis=-1, keepdims=True)
    spread = jnp.mean(center * center, axis=-1, keepdims=True)
    return center * lax.rsqrt(spread + EPSILON) * gain + bias


def normalize(pair, gain, bias):
    return layer_norm(pair.astype(jnp.float32), gain, bias).astype(jnp.bfloat16)


def project_all(pair, gain, bias, weight_in):
    projected = jnp.einsum(
        "ijc,cd->ijd", normalize(pair, gain, bias), weight_in, preferred_element_type=jnp.float32
    )
    left_operand = (jax.nn.sigmoid(projected[..., :CH]) * projected[..., CH : 2 * CH]).astype(
        jnp.bfloat16
    )
    right_operand = (
        jax.nn.sigmoid(projected[..., 2 * CH : 3 * CH]) * projected[..., 3 * CH : 4 * CH]
    ).astype(jnp.bfloat16)
    gating = jax.nn.sigmoid(projected[..., 4 * CH :])
    return (left_operand, right_operand, gating)


def finish(pair, mixed, gating, gain, bias, weight_out):
    normed = layer_norm(mixed, gain, bias).astype(jnp.bfloat16)
    update = gating * jnp.einsum(
        "ijc,cd->ijd", normed, weight_out, preferred_element_type=jnp.float32
    )
    return (pair.astype(jnp.float32) + update).astype(jnp.bfloat16)


def shards(
    pair,
    out_norm_gain,
    out_norm_bias,
    out_weight_in,
    out_mix_gain,
    out_mix_bias,
    out_weight_out,
    in_norm_gain,
    in_norm_bias,
    in_weight_in,
    in_mix_gain,
    in_mix_bias,
    in_weight_out,
):
    ratio = lax.axis_size("row") // lax.axis_size("col")
    row_index = lax.axis_index("row")
    col_index = lax.axis_index("col")
    rows = pair.shape[0]
    left_block, right_block, gating = project_all(pair, out_norm_gain, out_norm_bias, out_weight_in)
    left_rows, right_rows = (
        lax.all_gather(left_block, "col", axis=1, tiled=True),
        lax.all_gather(right_block, "col", axis=1, tiled=True),
    )
    right_far = jnp.concatenate(
        [spread_2(right_rows, "row", col_index * ratio + offset) for offset in range(ratio)], axis=0
    )
    mixed = jnp.einsum("ikc,jkc->ijc", left_rows, right_far, preferred_element_type=jnp.float32)
    first = finish(pair, mixed, gating, out_mix_gain, out_mix_bias, out_weight_out)
    start = row_index % ratio * rows
    left_block, right_block, gating = project_all(first, in_norm_gain, in_norm_bias, in_weight_in)
    left_cols, right_cols = (
        lax.all_gather(left_block, "row", axis=0, tiled=True),
        lax.all_gather(right_block, "row", axis=0, tiled=True),
    )
    left_far = spread_2(
        lax.dynamic_slice_in_dim(left_cols, start, rows, 1), "col", row_index // ratio
    )
    mixed = jnp.einsum("kic,kjc->ijc", left_far, right_cols, preferred_element_type=jnp.float32)
    return finish(first, mixed, gating, in_mix_gain, in_mix_bias, in_weight_out)


def solution(mesh):
    return jax.shard_map(
        shards,
        mesh=mesh,
        in_specs=(
            P("row", "col", None),
            P(),
            P(),
            P(),
            P(),
            P(),
            P(),
            P(),
            P(),
            P(),
            P(),
            P(),
            P(),
        ),
        out_specs=P("row", "col", None),
        check_vma=False,
    )
```

profile of v0, /device:TPU:1, one launch (start us, length us, event | category | flops | bytes accessed | tf_op | source)
XLA Modules:
  0.0 1039.3 jit_solution(356044462574241125)
XLA Ops:
  6.5 0.0 copy-start
  6.5 1.1 convert_reduce_fusion
  7.6 1.1 fusion.11
  8.8 0.0 copy-done
  8.8 1.3 fusion.39
  10.1 0.1 fusion.30
  10.2 0.7 copy.29
  10.9 0.0 all-gather.5.cloned.1.call-update
  10.9 0.0 all-gather.7.cloned.1.call-start
  11.0 0.7 copy.32
  11.7 0.0 all-gather.7.cloned.1.call-update
  11.7 0.0 all-reduce.6.cloned.1.call-start
  11.8 69.9 %all-gather.5.cloned.1.call-done = bf16[14,448,128]{2,0,1:T(8,128)(2,1)} async-done(((bf16[14,28,128]{2,0,1:T(8,128)(2,1)}), bf16[14,448,128]{2,0,1:T(8,128)(2,1)}) %all-gather.5.cloned.1.call-update) | async-done | bytes 1605648 | tf_op jit(solution)/shard_map/all_gather | solution.py:71
  81.7 3.9 copy.30
  85.6 2.3 broadcast_select_fusion.2
  87.9 0.0 all-reduce.6.cloned.1.call-update
  87.9 0.0 all-gather.11.cloned.1.call-start
  87.9 59.2 %all-gather.7.cloned.1.call-done = bf16[14,448,128]{2,0,1:T(8,128)(2,1)} async-done(((bf16[14,28,128]{2,0,1:T(8,128)(2,1)}), bf16[14,448,128]{2,0,1:T(8,128)(2,1)}) %all-gather.7.cloned.1.call-update) | async-done | bytes 1605648 | tf_op jit(solution)/shard_map/all_gather | solution.py:70
  147.2 3.9 copy.33
  151.0 319.4 %all-reduce.6.cloned.1.call-done = (bf16[14,448,128]{1,0,2:T(8,128)(2,1)}, bf16[14,448,128]{1,0,2:T(8,128)(2,1)}) async-done(((bf16[14,448,128]{1,0,2:T(8,128)(2,1)}, bf16[14,448,128]{1,0,2:T(8,128)(2,1)}), (bf16[14,448,128]{1,0,2:T(8,128)(2,1)}, bf16[14,448,128]{1,0,2:T(8,128)(2,1)})) %all-reduce.6.cloned.1.call-update) | async-done | bytes 3211280 | tf_op jit(solution)/shard_map/psum | solution.py:14
  470.5 4.5 fusion
  474.9 1.6 copy.34
  476.6 0.1 bitcast_reduce_fusion.1
  476.7 0.2 multiply_reduce_fusion.2
  477.0 0.0 copy-done.1
  477.0 0.0 copy-done.7
  477.0 1.0 fusion.61
  478.0 0.0 copy-start.2
  478.1 0.2 multiply_reduce_fusion.1
  478.4 0.4 fusion.37
  478.7 0.8 fusion.15
  479.6 0.0 all-gather.11.cloned.1.call-update
  479.6 0.0 all-gather.9.cloned.1.call-start
  479.6 0.5 all-gather.9.cloned.1.call-update
  480.2 0.0 all-reduce.4.cloned.1.call-start
  480.2 163.2 %all-gather.11.cloned.1.call-done = bf16[448,28,128]{2,1,0:T(8,128)(2,1)} async-done(((bf16[14,28,128]{2,1,0:T(8,128)(2,1)}), bf16[448,28,128]{2,1,0:T(8,128)(2,1)}) %all-gather.11.cloned.1.call-update) | async-done | bytes 3211280 | tf_op jit(solution)/shard_map/all_gather | solution.py:81
  643.4 3.9 constant_dynamic-slice_fusion
  647.4 3.9 copy.38
  651.2 1.5 broadcast_select_fusion
  652.7 0.0 all-reduce.4.cloned.1.call-update
  652.8 158.8 %all-gather.9.cloned.1.call-done = bf16[448,28,128]{2,1,0:T(8,128)(2,1)} async-done(((bf16[14,28,128]{2,1,0:T(8,128)(2,1)}), bf16[448,28,128]{2,1,0:T(8,128)(2,1)}) %all-gather.9.cloned.1.call-update) | async-done | bytes 3211280 | tf_op jit(solution)/shard_map/all_gather | solution.py:82
  811.6 22.0 %copy.36 = bf16[448,28,128]{1,0,2:T(8,128)(2,1)} copy(bf16[448,28,128]{2,1,0:T(8,128)(2,1)} %all-gather.9.cloned.1.call-done) | data formatting | bytes 6422528 | tf_op jit(solution)/shard_map/all_gather | solution.py:82
  833.6 189.8 %all-reduce.4.cloned.1.call-done = bf16[448,14,128]{0,1,2:T(8,128)(2,1)} async-done(((bf16[448,14,128]{0,1,2:T(8,128)(2,1)}), bf16[448,14,128]{0,1,2:T(8,128)(2,1)}) %all-reduce.4.cloned.1.call-update) | async-done | bytes 1605648 | tf_op jit(solution)/shard_map/psum | solution.py:14
  1023.5 7.2 fusion.62
  1030.6 0.4 copy.37
  1031.0 0.1 bitcast_reduce_fusion
  1031.2 0.2 multiply_reduce_fusion
  1031.5 1.0 fusion.7
  (26 shorter events, 0.1 us)
Async XLA Ops:
  6.5 2.3 copy-start
  6.5 75.2 %all-gather.5.cloned.1.call-start = ((), (), s32[]{:S(2)}) async-start(), calls=%async_computation | async-start | bytes 1949696 | tf_op jit(solution)/shard_map/all_gather | solution.py:71
  10.9 136.2 %all-gather.7.cloned.1.call-start = ((), (), s32[]{:S(2)}) async-start(), calls=%async_computation.1 | async-start | bytes 1949696 | tf_op jit(solution)/shard_map/all_gather | solution.py:70
  11.7 458.8 %all-reduce.6.cloned.1.call-start = ((), (), s32[]{:S(2)}) async-start(), calls=%async_computation.5 | async-start | bytes 8388608 | tf_op jit(solution)/shard_map/psum | solution.py:14
  87.9 555.5 %all-gather.11.cloned.1.call-start = ((), (), s32[]{:S(2)}) async-start(), calls=%async_computation.3 | async-start | bytes 3784704 | tf_op jit(solution)/shard_map/all_gather | solution.py:81
  470.5 6.5 copy-start.1
  470.5 6.5 copy-start.7
  474.9 3.4 copy-start.4
  474.9 3.4 copy-start.5
  474.9 3.4 copy-start.6
  478.0 165.4 %copy-start.2 = (f32[14,28,128]{2,1,0:T(8,128)}, f32[14,28,128]{2,1,0:T(8,128)S(1)}, u32[]{:S(2)}) copy-start(f32[14,28,128]{2,1,0:T(8,128)S(1)} %get-tuple-element.14) | copy-start | bytes 602116
  479.6 332.0 %all-gather.9.cloned.1.call-start = ((), (), s32[]{:S(2)}) async-start(), calls=%async_computation.2 | async-start | bytes 3784704 | tf_op jit(solution)/shard_map/all_gather | solution.py:82
  480.2 543.3 %all-reduce.4.cloned.1.call-start = ((), (), s32[]{:S(2)}) async-start(), calls=%async_computation.4 | async-start | bytes 4194304 | tf_op jit(solution)/shard_map/psum | solution.py:14
  833.6 197.8 %copy-start.3 = (f32[14,28,128]{2,1,0:T(8,128)S(1)}, f32[14,28,128]{2,1,0:T(8,128)}, u32[]{:S(2)}) copy-start(f32[14,28,128]{2,1,0:T(8,128)} %copy-done.2) | copy-start | bytes 602116
  833.6 197.8 %copy-start.8 = (bf16[128,128]{1,0:T(8,128)(2,1)S(1)}, bf16[128,128]{1,0:T(8,128)(2,1)}, u32[]{:S(2)}) copy-start(bf16[128,128]{1,0:T(8,128)(2,1)} %param.25) | copy-start | bytes 98308
  833.6 197.8 %copy-start.9 = (f32[128]{0:T(128)S(1)}, f32[128]{0:T(128)}, u32[]{:S(2)}) copy-start(f32[128]{0:T(128)} %param.24) | copy-start | bytes 1540
  833.6 197.9 %copy-start.10 = (f32[128]{0:T(128)S(1)}, f32[128]{0:T(128)}, u32[]{:S(2)}) copy-start(f32[128]{0:T(128)} %param.23) | copy-start | bytes 1540
Sparse Core Ops, SparseCore 0:
  11.1 70.6 all-gather.4
  85.0 62.0 all-gather.6
  150.1 320.2 all-reduce.5
  479.7 163.6 all-gather.10
  645.4 166.1 all-gather.8
  814.4 209.0 all-reduce.3
where the time goes:
time: 1040 us
  waiting for transfers between devices  961 us (92%)
  local copies, waits for them, and re-layouts  41.1 us (4%)
  matrix products  15.3 us (1%)
  between operations  13.8 us (1%)
    psum x2, waiting for transfers between devices, spread_2(): return lax.psum(kept, axis)  509 us
    all_gather x1, waiting for transfers between devices, shards(): lax.all_gather(left_block, 'row', axis=0, tiled=True)  163 us
    all_gather x1, waiting for transfers between devices, shards(): lax.all_gather(right_block, 'row', axis=0, tiled=True)  159 us
    all_gather x1, waiting for transfers between devices, shards(): lax.all_gather(right_block, 'col', axis=1, tiled=True)  69.9 us
    all_gather x1, waiting for transfers between devices, shards(): lax.all_gather(left_block, 'col', axis=1, tiled=True)  59.2 us
    all_gather x1, local copies, waits for them, and re-layouts, shards(): lax.all_gather(right_block, 'row', axis=0, tiled=True)  22 us
  transfers between devices with their start and end apart: 6, of which 6 were waited for; matrix products, arithmetic and copies ran while one was open for 4% of the time, Pallas kernels for 0%

commit v1 on v0

v1 whole, which is shorter than its diff:
```python
import jax
import jax.numpy as jnp
from jax import lax
from jax.sharding import Mesh, PartitionSpec as P

CH = 128
EPSILON = 1e-05

ROW = ("z", "ylo")
COL = ("yhi", "x", "core")
OUT_GROUP = ("z", "yhi", "x", "core")
IN_GROUP = ("z", "ylo", "yhi", "core")


def layer_norm(values, gain, bias):
    center = values - jnp.mean(values, axis=-1, keepdims=True)
    spread = jnp.mean(center * center, axis=-1, keepdims=True)
    return center * lax.rsqrt(spread + EPSILON) * gain + bias


def project_all(pair, gain, bias, weight_in):
    normed = layer_norm(pair.astype(jnp.float32), gain, bias).astype(jnp.bfloat16)
    projected = jnp.einsum("ijc,cd->ijd", normed, weight_in, preferred_element_type=jnp.float32)
    left = jax.nn.sigmoid(projected[..., :CH]) * projected[..., CH : 2 * CH]
    right = jax.nn.sigmoid(projected[..., 2 * CH : 3 * CH]) * projected[..., 3 * CH : 4 * CH]
    gating = jax.nn.sigmoid(projected[..., 4 * CH :])
    both = jnp.stack([left, right]).astype(jnp.bfloat16)
    return both.transpose(3, 0, 1, 2), gating


def finish(pair, mixed, gating, gain, bias, weight_out):
    normed = layer_norm(mixed, gain, bias).astype(jnp.bfloat16)
    update = gating * jnp.einsum(
        "ijc,cd->ijd", normed, weight_out, preferred_element_type=jnp.float32
    )
    return (pair.astype(jnp.float32) + update).astype(jnp.bfloat16)


def exchange(values, group):
    return lax.all_to_all(values, group, 0, 0, tiled=True)


def shards(pair, og, ob, owi, omg, omb, owo, ig, ib, iwi, img, imb, iwo):
    rows, cols, _ = pair.shape
    both, gating = project_all(pair, og, ob, owi)
    both = exchange(both, OUT_GROUP).reshape(8, 16, 2, rows, cols)
    both = both.transpose(2, 0, 3, 1, 4).reshape(2, 8, rows, 16 * cols)
    left = both[0].reshape(8 * rows, 16 * cols)
    right = lax.all_gather(both[1], "ylo", axis=1).reshape(32 * rows, 16 * cols)
    mixed = jnp.einsum("ik,jk->ij", left, right, preferred_element_type=jnp.float32)
    mixed = mixed.astype(jnp.bfloat16).reshape(8, rows, 16, cols).transpose(0, 2, 1, 3)
    mixed = exchange(mixed.reshape(128, rows, cols), OUT_GROUP)
    mixed = mixed.transpose(1, 2, 0).astype(jnp.float32)
    first = finish(pair, mixed, gating, omg, omb, owo)

    both, gating = project_all(first, ig, ib, iwi)
    both = exchange(both, IN_GROUP).reshape(32, 2, 2, 2, rows, cols)
    both = both.transpose(3, 0, 4, 1, 2, 5).reshape(2, 32 * rows, 2, 2, cols)
    left = lax.all_gather(both[0], "x", axis=2).reshape(32 * rows, 16 * cols)
    right = both[1].reshape(32 * rows, 4 * cols)
    mixed = jnp.einsum("ki,kj->ij", left, right, preferred_element_type=jnp.float32)
    mixed = mixed.astype(jnp.bfloat16).reshape(32, rows, 4, cols).transpose(0, 2, 1, 3)
    mixed = exchange(mixed.reshape(128, rows, cols), IN_GROUP)
    mixed = mixed.transpose(1, 2, 0).astype(jnp.float32)
    return finish(first, mixed, gating, img, imb, iwo)


def solution(mesh):
    fine = Mesh(mesh.devices.reshape(8, 4, 2, 4, 2), ("z", "ylo", "yhi", "x", "core"))
    return jax.shard_map(
        shards,
        mesh=fine,
        in_specs=(P(ROW, COL, None),) + (P(),) * 12,
        out_specs=P(ROW, COL, None),
        check_vma=False,
    )
```

time: 1040 us -> 149 us (0.14)
  waiting for transfers between devices: 961 us -> 0 us
  blocking collectives: 0 us -> 126 us
  local copies, waits for them, and re-layouts: 41.1 us -> 15.2 us
  between operations: 13.8 us -> 0.52 us
  matrix products: 15.3 us -> 3.56 us
    psum x2 -> x0, waiting for transfers between devices: 509 us -> none  [spread_2(): return lax.psum(kept, axis)]
    all_gather x4 -> x0, waiting for transfers between devices: 451 us -> none  [the longest x1 163 us: shards(): lax.all_gather(left_block, 'row', axis=0, tiled=True)]
    all_to_all x0 -> x4, blocking collectives: none -> 102 us  [exchange(): return lax.all_to_all(values, group, 0, 0, tiled=True)]
    all_gather x3 -> x2, local copies, waits for them, and re-layouts: 29.8 us -> 0.2 us  [the longest x1 0.14 us: shards(): right = lax.all_gather(both[1], 'ylo', axis=1).reshape(32 * rows, 16 * cols)]
    all_gather x0 -> x2, blocking collectives: none -> 24 us  [the longest x1 13.6 us: shards(): right = lax.all_gather(both[1], 'ylo', axis=1).reshape(32 * rows, 16 * cols)]
    dot_general x4, matrix products: 13.3 us -> 2.23 us  [the longest x2 1.67 us: project_all(): jnp.einsum('ijc,cd->ijd', normed, weight_in, preferred_element_type=jnp.f...]
  transfers between devices with their start and end apart: 6 -> 0, of which waited for: 6 -> 0; matrix products, arithmetic and copies ran while one was open for 4% -> 0% of each run, Pallas kernels for 0% -> 0%
where the time goes in v1:
time: 149 us
  blocking collectives  126 us (85%)
  local copies, waits for them, and re-layouts  15.2 us (10%)
  other arithmetic  3.58 us (2%)
  matrix products  3.56 us (2%)
    all_to_all x4, blocking collectives, exchange(): return lax.all_to_all(values, group, 0, 0, tiled=True)  102 us
    all_gather x1, blocking collectives, shards(): right = lax.all_gather(both[1], 'ylo', axis=1).reshape(32 * rows, 16 * cols)  13.6 us
    all_gather x1, blocking collectives, shards(): left = lax.all_gather(both[0], 'x', axis=2).reshape(32 * rows, 16 * cols)  10.3 us
    unnamed x30, local copies, waits for them, and re-layouts  5.98 us

profile of v1, /device:TPU:1, one launch (start us, length us, event | category | flops | bytes accessed | tf_op | source)
XLA Modules:
  0.0 148.6 jit_solution(15909813351887191790)
XLA Ops:
  0.0 1.1 convert_reduce_fusion
  1.1 1.1 fusion.7
  2.3 1.3 fusion.47
  3.7 1.1 copy.59
  4.9 0.8 reshape.102
  5.6 36.8 %all_to_all.20 = bf16[128,2,392]{2,1,0:T(2,128)(2,1)S(1)} all-to-all(bf16[128,2,392]{2,1,0:T(2,128)(2,1)S(1)} %reshape.102), channel_id=1, replica_groups=mesh['z'=8,'ylo'=4,'yhi'=2,'x'=4,'core'=2] {'z','yhi','x','core'}, dimensions={0} | all-to-all | bytes 401408 | tf_op jit(solution)/shard_map/all_to_all | solution.py:40
  42.5 1.2 reshape.103
  43.7 0.2 copy.60
  43.9 0.3 fusion.75
  44.2 0.4 all_gather_squeeze.6
  44.6 13.6 %all_gather.6 = bf16[8,4,14,448]{3,0,2,1:T(8,128)(2,1)S(1)} all-gather(bf16[8,1,14,448]{3,0,2,1:T(8,128)(2,1)S(1)} %all_gather_squeeze.6), channel_id=1, replica_groups=mesh['z'=8,'ylo'=4,'yhi'=2,'x'=4,'core'=2] {'ylo'}, dimensions={1}, use_global_device_ids=true | all-gather | bytes 501760 | tf_op jit(solution)/shard_map/all_gather | solution.py:49
  58.2 0.1 copy.62
  58.4 0.2 reshape.91
  58.6 0.4 reshape_squeeze.6
  59.1 0.3 convolution_convert_fusion.1
  59.3 0.6 reshape.92
  60.0 0.3 copy.64
  60.4 0.6 reshape.104
  60.9 24.0 %all_to_all.21 = bf16[128,2,196]{2,1,0:T(2,128)(2,1)S(1)} all-to-all(bf16[128,2,196]{2,1,0:T(2,128)(2,1)S(1)} %reshape.104), channel_id=1, replica_groups=mesh['z'=8,'ylo'=4,'yhi'=2,'x'=4,'core'=2] {'z','yhi','x','core'}, dimensions={0} | all-to-all | bytes 200704 | tf_op jit(solution)/shard_map/all_to_all | solution.py:40
  84.9 0.4 reshape.105
  85.3 0.4 copy.65
  85.9 0.2 fusion.41
  86.2 0.4 fusion.76
  86.6 0.3 multiply_reduce_fusion
  86.9 0.4 fusion.45
  87.5 1.1 copy.66
  88.6 0.8 reshape.106
  89.4 19.9 %all_to_all.22 = bf16[128,2,392]{2,1,0:T(2,128)(2,1)S(1)} all-to-all(bf16[128,2,392]{2,1,0:T(2,128)(2,1)S(1)} %reshape.106), channel_id=1, replica_groups=mesh['z'=8,'ylo'=4,'yhi'=2,'x'=4,'core'=2] {'z','ylo','yhi','core'}, dimensions={0} | all-to-all | bytes 401408 | tf_op jit(solution)/shard_map/all_to_all | solution.py:40
  109.2 1.2 reshape.107
  110.5 0.2 copy.67
  110.7 0.7 fusion.74
  111.4 0.3 copy.71
  111.7 0.2 reshape_squeeze.7
  112.0 0.3 copy.68
  112.3 0.7 copy.69
  113.0 10.3 %all_gather.7 = bf16[448,2,4,2,28]{0,3,4,1,2:T(2,128)(2,1)S(1)} all-gather(bf16[448,2,1,2,28]{0,3,4,1,2:T(2,128)(2,1)S(1)} %copy.69), channel_id=1, replica_groups=mesh['z'=8,'ylo'=4,'yhi'=2,'x'=4,'core'=2] {'x'}, dimensions={2}, use_global_device_ids=true | all-gather | bytes 501760 | tf_op jit(solution)/shard_map/all_gather | solution.py:59
  123.4 0.2 reshape.95
  123.6 0.3 convolution_convert_fusion
  123.9 0.2 reshape.96
  124.1 0.2 copy.72
  124.3 0.3 copy.73
  124.6 0.6 reshape.108
  125.2 21.2 %all_to_all.23 = bf16[128,2,196]{2,1,0:T(2,128)(2,1)S(1)} all-to-all(bf16[128,2,196]{2,1,0:T(2,128)(2,1)S(1)} %reshape.108), channel_id=1, replica_groups=mesh['z'=8,'ylo'=4,'yhi'=2,'x'=4,'core'=2] {'z','ylo','yhi','core'}, dimensions={0} | all-to-all | bytes 200704 | tf_op jit(solution)/shard_map/all_to_all | solution.py:40
  146.4 0.4 reshape.109
  146.8 0.4 copy.74
  147.2 0.1 bitcast_reduce_fusion
  147.4 0.2 fusion.35
  147.7 1.0 fusion.3
  (38 shorter events, 0.7 us)
Async XLA Ops:
  0.0 2.2 %copy-start = (bf16[128,640]{1,0:T(8,128)(2,1)S(1)}, bf16[128,640]{1,0:T(8,128)(2,1)}, u32[]{:S(2)}) copy-start(bf16[128,640]{1,0:T(8,128)(2,1)} %param.16) | copy-start | bytes 491524
  60.3 25.9 %copy-start.1 = (bf16[14,28,128]{2,1,0:T(8,128)(2,1)S(1)}, bf16[14,28,128]{2,1,0:T(8,128)(2,1)}, u32[]{:S(2)}) copy-start(bf16[14,28,128]{2,1,0:T(8,128)(2,1)} %param.13) | copy-start | bytes 301060
  60.3 25.9 %copy-start.5 = (bf16[128,128]{1,0:T(8,128)(2,1)S(1)}, bf16[128,128]{1,0:T(8,128)(2,1)}, u32[]{:S(2)}) copy-start(bf16[128,128]{1,0:T(8,128)(2,1)} %param.19) | copy-start | bytes 98308
  60.4 25.9 %copy-start.7 = (f32[128]{0:T(128)S(1)}, f32[128]{0:T(128)}, u32[]{:S(2)}) copy-start(f32[128]{0:T(128)} %param.18) | copy-start | bytes 1540
  60.4 25.9 %copy-start.8 = (f32[128]{0:T(128)S(1)}, f32[128]{0:T(128)}, u32[]{:S(2)}) copy-start(f32[128]{0:T(128)} %param.17) | copy-start | bytes 1540
  85.8 1.1 copy-start.2
  85.8 1.1 copy-start.3
  85.8 1.1 copy-start.4
  124.6 23.0 %copy-start.6 = (bf16[128,128]{1,0:T(8,128)(2,1)S(1)}, bf16[128,128]{1,0:T(8,128)(2,1)}, u32[]{:S(2)}) copy-start(bf16[128,128]{1,0:T(8,128)(2,1)} %param.25) | copy-start | bytes 98308
  124.6 23.0 %copy-start.9 = (f32[128]{0:T(128)S(1)}, f32[128]{0:T(128)}, u32[]{:S(2)}) copy-start(f32[128]{0:T(128)} %param.24) | copy-start | bytes 1540
  124.6 23.0 %copy-start.10 = (f32[128]{0:T(128)S(1)}, f32[128]{0:T(128)}, u32[]{:S(2)}) copy-start(f32[128]{0:T(128)} %param.23) | copy-start | bytes 1540

commit v2 on v1

--- a/solution.py
+++ b/solution.py
@@ -6,10 +6,10 @@
 CH = 128
 EPSILON = 1e-05
 
-ROW = ("z", "ylo")
-COL = ("yhi", "x", "core")
-OUT_GROUP = ("z", "yhi", "x", "core")
-IN_GROUP = ("z", "ylo", "yhi", "core")
+AXES = ("zh", "zl", "ylo", "yhi", "xh", "xl", "core")
+ROW, COL = AXES[:3], AXES[3:]
+OUT_GROUP = ("zh", "ylo", "yhi", "xh", "xl")
+IN_GROUP = ("zh", "zl", "ylo", "yhi", "xl")
 
 
 def layer_norm(values, gain, bias):
@@ -43,22 +43,24 @@
 def shards(pair, og, ob, owi, omg, omb, owo, ig, ib, iwi, img, imb, iwo):
     rows, cols, _ = pair.shape
     both, gating = project_all(pair, og, ob, owi)
-    both = exchange(both, OUT_GROUP).reshape(8, 16, 2, rows, cols)
-    both = both.transpose(2, 0, 3, 1, 4).reshape(2, 8, rows, 16 * cols)
-    left = both[0].reshape(8 * rows, 16 * cols)
-    right = lax.all_gather(both[1], "ylo", axis=1).reshape(32 * rows, 16 * cols)
-    mixed = jnp.einsum("ik,jk->ij", left, right, preferred_element_type=jnp.float32)
-    mixed = mixed.astype(jnp.bfloat16).reshape(8, rows, 16, cols).transpose(0, 2, 1, 3)
+    both = exchange(both, OUT_GROUP).reshape(16, 8, 2, rows, cols)
+    both = both.transpose(2, 0, 3, 1, 4).reshape(2, 16 * rows, 8 * cols)
+    left = lax.all_gather(both[0], "core", axis=0)
+    right = lax.all_gather(both[1], ("zl", "core"), axis=0)
+    right = right.reshape(2, 2, 4, 2, 2 * rows, 8 * cols)
+    right = lax.dynamic_index_in_dim(right, lax.axis_index("core"), 3, keepdims=False)
+    mixed = jnp.einsum("hik,zhwjk->iwzj", left, right, preferred_element_type=jnp.float32)
+    mixed = mixed.astype(jnp.bfloat16).reshape(16, rows, 8, cols).transpose(0, 2, 1, 3)
     mixed = exchange(mixed.reshape(128, rows, cols), OUT_GROUP)
     mixed = mixed.transpose(1, 2, 0).astype(jnp.float32)
     first = finish(pair, mixed, gating, omg, omb, owo)
 
     both, gating = project_all(first, ig, ib, iwi)
-    both = exchange(both, IN_GROUP).reshape(32, 2, 2, 2, rows, cols)
-    both = both.transpose(3, 0, 4, 1, 2, 5).reshape(2, 32 * rows, 2, 2, cols)
-    left = lax.all_gather(both[0], "x", axis=2).reshape(32 * rows, 16 * cols)
-    right = both[1].reshape(32 * rows, 4 * cols)
-    mixed = jnp.einsum("ki,kj->ij", left, right, preferred_element_type=jnp.float32)
+    both = exchange(both, IN_GROUP).reshape(32, 4, 2, rows, cols)
+    both = both.transpose(2, 0, 3, 1, 4).reshape(2, 32 * rows, 4 * cols)
+    left = lax.all_gather(both[0], ("xh", "core"), axis=0)
+    left = left.reshape(2, 2, 32 * rows, 2, 2, cols)
+    mixed = jnp.einsum("xhkylc,kj->yxlhcj", left, both[1], preferred_element_type=jnp.float32)
     mixed = mixed.astype(jnp.bfloat16).reshape(32, rows, 4, cols).transpose(0, 2, 1, 3)
     mixed = exchange(mixed.reshape(128, rows, cols), IN_GROUP)
     mixed = mixed.transpose(1, 2, 0).astype(jnp.float32)
@@ -66,7 +68,7 @@
 
 
 def solution(mesh):
-    fine = Mesh(mesh.devices.reshape(8, 4, 2, 4, 2), ("z", "ylo", "yhi", "x", "core"))
+    fine = Mesh(mesh.devices.reshape(4, 2, 4, 2, 2, 2, 2), AXES)
     return jax.shard_map(
         shards,
         mesh=fine,

time: 149 us -> 135 us (0.906)
  blocking collectives: 126 us -> 77.4 us
  starting transfers between devices: 0 us -> 20.8 us
  waiting for transfers between devices: 0 us -> 13.7 us
    all_to_all x4 -> x3, blocking collectives: 102 us -> 55.3 us  [exchange(): return lax.all_to_all(values, group, 0, 0, tiled=True)]
    all_to_all x0 -> x1, starting transfers between devices: none -> 20.8 us  [exchange(): return lax.all_to_all(values, group, 0, 0, tiled=True)]
    all_to_all x0 -> x1, waiting for transfers between devices: none -> 13.7 us  [exchange(): return lax.all_to_all(values, group, 0, 0, tiled=True)]
    all_gather x2 -> x3, blocking collectives: 24 us -> 22.1 us  [the longest x1 10.6 us: shards(): left = lax.all_gather(both[0], ('xh', 'core'), axis=0)]
    another operation x4 -> x0, local copies, waits for them, and re-layouts: 1.79 us -> none  [the longest x1 0.69 us: shards(): left = lax.all_gather(both[0], 'x', axis=2).reshape(32 * rows, 16 * cols)]
  transfers between devices with their start and end apart: 0 -> 1, of which waited for: 0 -> 1; matrix products, arithmetic and copies ran while one was open for 0% -> 0% of each run, Pallas kernels for 0% -> 0%
where the time goes in v2:
time: 135 us; the launch traced here: 134 us
  blocking collectives  77.4 us (57%)
  starting transfers between devices  20.8 us (15%)
  local copies, waits for them, and re-layouts  14.5 us (11%)
  waiting for transfers between devices  13.7 us (10%)
  other arithmetic  3.58 us (3%)
  matrix products  3.56 us (3%)
    all_to_all x3, blocking collectives, exchange(): return lax.all_to_all(values, group, 0, 0, tiled=True)  55.3 us
    all_to_all x1, starting transfers between devices, exchange(): return lax.all_to_all(values, group, 0, 0, tiled=True)  20.8 us
    all_to_all x1, waiting for transfers between devices, exchange(): return lax.all_to_all(values, group, 0, 0, tiled=True)  13.7 us
    all_gather x1, blocking collectives, shards(): left = lax.all_gather(both[0], ('xh', 'core'), axis=0)  10.6 us
    all_gather x1, blocking collectives, shards(): right = lax.all_gather(both[1], ('zl', 'core'), axis=0)  6.99 us
    unnamed x30, local copies, waits for them, and re-layouts  6.68 us
    all_gather x1, blocking collectives, shards(): left = lax.all_gather(both[0], 'core', axis=0)  4.47 us
  transfers between devices with their start and end apart: 1, of which 1 were waited for; matrix products, arithmetic and copies ran while one was open for 0% of the time, Pallas kernels for 0%

profile of v2, /device:TPU:1, one launch (start us, length us, event | category | flops | bytes accessed | tf_op | source)
XLA Modules:
  0.0 134.1 jit_solution(5880166797498042500)
XLA Ops:
  0.0 1.1 convert_reduce_fusion
  1.1 1.1 fusion.10
  2.3 1.3 fusion.51
  3.7 1.1 copy.91
  4.9 1.5 %reshape.105 = bf16[128,2,392]{2,1,0:T(2,128)(2,1)} reshape(bf16[128,14,2,28]{3,2,1,0:T(2,128)(2,1)S(1)} %bitcast.113) | data formatting | bytes 401408
  6.3 20.8 %all-to-all-start = ((bf16[128,2,392]{2,1,0:T(2,128)(2,1)}), bf16[128,2,392]{2,1,0:T(2,128)(2,1)S(1)}, u32[]{:S(2)}, u32[]{:S(2)}) async-start(bf16[128,2,392]{2,1,0:T(2,128)(2,1)} %reshape.105), calls=%async_computation | async-start | bytes 524288 | tf_op jit(solution)/shard_map/all_to_all | solution.py:40
  27.1 13.7 %all-to-all-done = bf16[128,2,392]{2,1,0:T(2,128)(2,1)S(1)} async-done(((bf16[128,2,392]{2,1,0:T(2,128)(2,1)}), bf16[128,2,392]{2,1,0:T(2,128)(2,1)S(1)}, u32[]{:S(2)}, u32[]{:S(2)}) %all-to-all-start) | async-done | bytes 200736 | tf_op jit(solution)/shard_map/all_to_all | solution.py:40
  40.8 1.2 reshape.106
  42.1 0.2 copy.123
  42.4 0.3 slice.60
  42.8 4.5 %all_gather.10 = bf16[2,224,224]{2,1,0:T(8,128)(2,1)S(1)} all-gather(bf16[1,224,224]{2,1,0:T(8,128)(2,1)S(1)} %slice.60), channel_id=1, replica_groups=mesh['zh'=4,'zl'=2,'ylo'=4,'yhi'=2,'xh'=2,'xl'=2,'core'=2] {'core'}, dimensions={0}, use_global_device_ids=true | all-gather | bytes 301056 | tf_op jit(solution)/shard_map/all_gather | solution.py:48
  47.3 0.3 slice.58
  47.6 7.0 %all_gather.9 = bf16[4,224,224]{2,1,0:T(8,128)(2,1)S(1)} all-gather(bf16[1,224,224]{2,1,0:T(8,128)(2,1)S(1)} %slice.58), channel_id=1, replica_groups=mesh['zh'=4,'zl'=2,'ylo'=4,'yhi'=2,'xh'=2,'xl'=2,'core'=2] {'zl','core'}, dimensions={0}, use_global_device_ids=true | all-gather | bytes 501760 | tf_op jit(solution)/shard_map/all_gather | solution.py:49
  54.7 0.3 fusion.6
  55.0 0.5 copy.97
  55.7 0.3 copy.99
  56.0 0.6 reshape.107
  56.6 19.1 %all_to_all.20 = bf16[128,2,196]{2,1,0:T(2,128)(2,1)S(1)} all-to-all(bf16[128,2,196]{2,1,0:T(2,128)(2,1)S(1)} %reshape.107), channel_id=1, replica_groups=mesh['zh'=4,'zl'=2,'ylo'=4,'yhi'=2,'xh'=2,'xl'=2,'core'=2] {'zh','ylo','..., dimensions={0} | all-to-all | bytes 200704 | tf_op jit(solution)/shard_map/all_to_all | solution.py:40
  75.7 0.4 reshape.108
  76.1 0.4 copy.100
  76.5 0.1 bitcast_reduce_fusion.1
  76.7 0.2 fusion.45
  77.0 0.4 fusion.81
  77.4 0.3 multiply_reduce_fusion
  77.7 0.4 fusion.49
  78.2 1.1 copy.101
  79.4 0.8 reshape.109
  80.1 19.3 %all_to_all.21 = bf16[128,2,392]{2,1,0:T(2,128)(2,1)S(1)} all-to-all(bf16[128,2,392]{2,1,0:T(2,128)(2,1)S(1)} %reshape.109), channel_id=1, replica_groups=mesh['zh'=4,'zl'=2,'ylo'=4,'yhi'=2,'xh'=2,'xl'=2,'core'=2] {'zh','zl','y..., dimensions={0} | all-to-all | bytes 401408 | tf_op jit(solution)/shard_map/all_to_all | solution.py:40
  99.4 1.2 reshape.110
  100.7 0.2 copy.102
  100.9 0.5 fusion.79
  101.4 0.2 copy.103
  101.5 0.2 reshape.100
  101.8 0.2 copy.104
  102.0 0.2 slice.68
  102.2 10.6 %all_gather.11 = bf16[4,448,112]{2,1,0:T(8,128)(2,1)S(1)} all-gather(bf16[1,448,112]{2,1,0:T(8,128)(2,1)S(1)} %slice.68), channel_id=1, replica_groups=mesh['zh'=4,'zl'=2,'ylo'=4,'yhi'=2,'xh'=2,'xl'=2,'core'=2] {'xh','core'}, dimensions={0}, use_global_device_ids=true | all-gather | bytes 501760 | tf_op jit(solution)/shard_map/all_gather | solution.py:61
  112.9 0.2 copy.115
  113.2 0.3 fusion.7
  113.5 0.2 reshape.93
  113.8 0.2 copy.108
  114.0 0.3 copy.109
  114.3 0.6 reshape.111
  114.9 16.9 %all_to_all.22 = bf16[128,2,196]{2,1,0:T(2,128)(2,1)S(1)} all-to-all(bf16[128,2,196]{2,1,0:T(2,128)(2,1)S(1)} %reshape.111), channel_id=1, replica_groups=mesh['zh'=4,'zl'=2,'ylo'=4,'yhi'=2,'xh'=2,'xl'=2,'core'=2] {'zh','zl','y..., dimensions={0} | all-to-all | bytes 200704 | tf_op jit(solution)/shard_map/all_to_all | solution.py:40
  131.8 0.4 reshape.112
  132.2 0.4 copy.110
  132.7 0.1 bitcast_reduce_fusion
  132.8 0.2 fusion.39
  133.1 1.0 fusion.4
  (41 shorter events, 1.0 us)
Async XLA Ops:
  0.0 2.2 %copy-start = (bf16[128,640]{1,0:T(8,128)(2,1)S(1)}, bf16[128,640]{1,0:T(8,128)(2,1)}, u32[]{:S(2)}) copy-start(bf16[128,640]{1,0:T(8,128)(2,1)} %param.16) | copy-start | bytes 491524
  6.3 34.5 %all-to-all-start = ((bf16[128,2,392]{2,1,0:T(2,128)(2,1)}), bf16[128,2,392]{2,1,0:T(2,128)(2,1)S(1)}, u32[]{:S(2)}, u32[]{:S(2)}) async-start(bf16[128,2,392]{2,1,0:T(2,128)(2,1)} %reshape.105), calls=%async_computation | async-start | bytes 524288 | tf_op jit(solution)/shard_map/all_to_all | solution.py:40
  56.0 21.0 %copy-start.1 = (bf16[14,28,128]{2,1,0:T(8,128)(2,1)S(1)}, bf16[14,28,128]{2,1,0:T(8,128)(2,1)}, u32[]{:S(2)}) copy-start(bf16[14,28,128]{2,1,0:T(8,128)(2,1)} %param.13) | copy-start | bytes 301060
  56.0 21.0 %copy-start.5 = (bf16[128,128]{1,0:T(8,128)(2,1)S(1)}, bf16[128,128]{1,0:T(8,128)(2,1)}, u32[]{:S(2)}) copy-start(bf16[128,128]{1,0:T(8,128)(2,1)} %param.19) | copy-start | bytes 98308
  56.0 21.0 %copy-start.7 = (f32[128]{0:T(128)S(1)}, f32[128]{0:T(128)}, u32[]{:S(2)}) copy-start(f32[128]{0:T(128)} %param.18) | copy-start | bytes 1540
  56.0 21.0 %copy-start.8 = (f32[128]{0:T(128)S(1)}, f32[128]{0:T(128)}, u32[]{:S(2)}) copy-start(f32[128]{0:T(128)} %param.17) | copy-start | bytes 1540
  76.5 1.1 copy-start.2
  76.5 1.1 copy-start.3
  76.5 1.1 copy-start.4
  114.3 18.8 %copy-start.6 = (bf16[128,128]{1,0:T(8,128)(2,1)S(1)}, bf16[128,128]{1,0:T(8,128)(2,1)}, u32[]{:S(2)}) copy-start(bf16[128,128]{1,0:T(8,128)(2,1)} %param.25) | copy-start | bytes 98308
  114.3 18.8 %copy-start.9 = (f32[128]{0:T(128)S(1)}, f32[128]{0:T(128)}, u32[]{:S(2)}) copy-start(f32[128]{0:T(128)} %param.24) | copy-start | bytes 1540
  114.3 18.8 %copy-start.10 = (f32[128]{0:T(128)S(1)}, f32[128]{0:T(128)}, u32[]{:S(2)}) copy-start(f32[128]{0:T(128)} %param.23) | copy-start | bytes 1540

commit v3 on v2

v3 whole, which is shorter than its diff:
```python
import jax
import jax.numpy as jnp
from jax import lax
from jax.experimental import pallas as pl
from jax.experimental.pallas import tpu as pltpu
from jax.sharding import Mesh, PartitionSpec as P

CH = 128
EPSILON = 1e-05
ROWS, COLS = 14, 28
F32, BF16 = jnp.float32, jnp.bfloat16

AXES = ("zh", "zl", "ylo", "yhi", "xh", "xl", "core")
ROW, COL = AXES[:3], AXES[3:]
OUT_GROUP = ("yhi", "xh", "xl", "zh", "ylo")
IN_GROUP = ("yhi", "xl", "zh", "zl", "ylo")
OUT_SHAPE, IN_SHAPE = (8, 16), (4, 32)


NT = (((1,), (1,)), ((), ()))
TN = (((0,), (1,)), ((), ()))


def dot(a, b, dims=(((1,), (0,)), ((), ()))):
    return lax.dot_general(a, b, dims, preferred_element_type=F32)


def iota(shape, axis):
    return lax.broadcasted_iota(jnp.int32, shape, axis)


def residue_of_slot(slot):
    inner = slot % 16
    residue = inner % 4 * 4 + inner // 4
    return jnp.where(residue < ROWS, slot // 16 * ROWS + residue, -1)


def transpose_groups(blocks):
    lane = iota(blocks[0].shape, 1)
    low, even = lane < 64, lane // 32 % 2 == 0
    a, b, c, d = blocks
    a, c = jnp.where(low, a, pltpu.roll(c, 64, 1)), jnp.where(low, pltpu.roll(a, 64, 1), c)
    b, d = jnp.where(low, b, pltpu.roll(d, 64, 1)), jnp.where(low, pltpu.roll(b, 64, 1), d)
    a, b = jnp.where(even, a, pltpu.roll(b, 32, 1)), jnp.where(even, pltpu.roll(a, 96, 1), b)
    c, d = jnp.where(even, c, pltpu.roll(d, 32, 1)), jnp.where(even, pltpu.roll(c, 96, 1), d)
    return [a, b, c, d]


def layer_norm(values, gain, bias):
    center = values - jnp.mean(values, axis=-1, keepdims=True)
    spread = jnp.mean(center * center, axis=-1, keepdims=True)
    return center * lax.rsqrt(spread + EPSILON) * gain + bias


def project(q, values, gain, bias, weight, stage, gate):
    normed = layer_norm(values, gain[...], bias[...]).astype(BF16)
    lane = iota((CH, 128), 1)
    valid = (lane // 32 * 4 + q < ROWS) & (residue_of_slot(lane % 32) >= 0)
    for side in range(2):
        opened = dot(weight[:, 2 * side * CH : (2 * side + 1) * CH], normed, TN)
        value = dot(weight[:, (2 * side + 1) * CH : (2 * side + 2) * CH], normed, TN)
        operand = jnp.where(valid, jax.nn.sigmoid(opened) * value, 0.0)
        stage[pl.ds(2 * q + side, CH, stride=8), :] = operand
    gate[128 * q : 128 * (q + 1), :] = jax.nn.sigmoid(dot(normed, weight[:, 4 * CH :]))


def finish(q, pair, mixed, gate, gain, bias, weight):
    values = mixed[pl.ds(q, CH, stride=4), :].T
    normed = layer_norm(values, gain[...], bias[...]).astype(BF16)
    rows = slice(128 * q, 128 * (q + 1))
    return (pair[rows, :].astype(F32) + gate[rows, :] * dot(normed, weight[...])).astype(BF16)


def open_kernel(pair, gain, bias, weight, sent, gate, spread, stage):
    place = (residue_of_slot(iota((32, COLS), 0)) == iota((32, COLS), 1)).astype(BF16)
    for q in range(4):
        parts = [
            dot(place, pair[4 * g + q]) if 4 * g + q < ROWS else jnp.zeros((32, CH), F32)
            for g in range(4)
        ]
        values = jnp.concatenate(parts, axis=0)
        spread[128 * q : 128 * (q + 1), :] = values.astype(BF16)
        project(q, values, gain, bias, weight, stage, gate)
    sent[...] = stage[...].astype(BF16)


def middle_kernel(
    pair, got, gate, mix_gain, mix_bias, weight_out, gain, bias, weight, sent, first, gate_in, mixed, stage
):
    mixed[...] = got[...].astype(F32)
    for q in range(4):
        values = finish(q, pair, mixed, gate, mix_gain, mix_bias, weight_out)
        first[128 * q : 128 * (q + 1), :] = values
        project(q, values.astype(F32), gain, bias, weight, stage, gate_in)
    sent[...] = stage[...].astype(BF16)


def close_kernel(first, got, gate, mix_gain, mix_bias, weight_out, updated, mixed):
    mixed[...] = got[...].astype(F32)
    place = (residue_of_slot(iota((COLS, 32), 1)) == iota((COLS, 32), 0)).astype(BF16)
    for q in range(4):
        values = finish(q, first, mixed, gate, mix_gain, mix_bias, weight_out)
        for g in range(4):
            if 4 * g + q < ROWS:
                updated[4 * g + q] = dot(place, values[32 * g : 32 * (g + 1)]).astype(BF16)


def split_kernel_out(got, left, right, stage, order):
    cols, rows = OUT_SHAPE
    size = rows * 8
    for half in range(2):
        lanes = slice(128 * half, 128 * (half + 1))
        first = 4 * half
        blocks = [got[size * (first + c) : size * (first + c + 1), :].astype(F32) for c in range(4)]
        for g, block in enumerate(transpose_groups(blocks)):
            stage[...] = block
            left[64 * g : 64 * (g + 1), lanes] = stage[pl.ds(0, 64, stride=2), :].astype(BF16)
            order[pl.ds(g, 64, stride=4), :] = stage[pl.ds(1, 64, stride=2), :]
        for zh in range(4):
            for yb in range(2):
                source, target = 32 * (2 * zh + yb), 32 * (4 * yb + zh)
                right[target : target + 32, lanes] = order[source : source + 32, :].astype(BF16)


def product_kernel_out(left, right, sent):
    core = lax.axis_index("core")
    for zl in range(2):
        mixed = jnp.zeros((256, 128), F32)
        for half in range(2):
            start = pl.multiple_of((2 * zl + half) * 256 + core * 128, 128)
            mixed += dot(left[256 * half : 256 * (half + 1), :], right[pl.ds(start, 128), :], NT)
        blocks = [mixed[64 * g : 64 * (g + 1)] for g in range(4)]
        for zh, block in enumerate(transpose_groups(blocks)):
            target = 64 * (2 * zh + zl)
            sent[target : target + 64, :] = block.astype(BF16)


def split_kernel_in(got, left, right, stage):
    blocks = [got[256 * c : 256 * (c + 1), :].astype(F32) for c in range(4)]
    for g, block in enumerate(transpose_groups(blocks)):
        stage[...] = block
        rows = slice(128 * g, 128 * (g + 1))
        left[:, rows] = stage[pl.ds(0, 128, stride=2), :].T.astype(BF16)
        right[rows, :] = stage[pl.ds(1, 128, stride=2), :].astype(BF16)


def product_kernel_in(left, right, sent, stage):
    for xh in range(2):
        for core in range(2):
            start = 128 * (2 * xh + core)
            mixed = dot(left[start : start + 128, :], right[...])
            for yhi in range(2):
                for xl in range(2):
                    source = 32 * (2 * yhi + xl)
                    target = 32 * (8 * yhi + 4 * xh + 2 * xl + core)
                    stage[target : target + 32, :] = mixed[source : source + 32]
    blocks = [stage[pl.ds(g, 128, stride=4), :] for g in range(4)]
    for c, block in enumerate(transpose_groups(blocks)):
        sent[128 * c : 128 * (c + 1), :] = block.astype(BF16)


def call(kernel, outs, scratch, *operands):
    whole = pl.BlockSpec(memory_space=pltpu.VMEM)
    outs = [jax.ShapeDtypeStruct(shape, kind) for shape, kind in outs]
    return pl.pallas_call(
        kernel,
        out_shape=outs,
        in_specs=[whole] * len(operands),
        out_specs=[whole] * len(outs),
        scratch_shapes=[pltpu.VMEM(shape, F32) for shape in scratch],
        compiler_params=pltpu.CompilerParams(vmem_limit_bytes=32 * 1024 * 1024),
    )(*operands)


def exchange(values, group):
    size = values.shape[0] // 128
    got = lax.all_to_all(values.reshape(128, size, 128), group, 0, 0, tiled=True)
    return got.reshape(values.shape)


def shards(pair, og, ob, owi, omg, omb, owo, ig, ib, iwi, img, imb, iwo):
    og, ob, omg, omb, ig, ib, img, imb = (v.reshape(1, CH) for v in (og, ob, omg, omb, ig, ib, img, imb))
    sent, gate, pair = call(
        open_kernel,
        [((1024, 128), BF16), ((512, CH), F32), ((512, CH), BF16)],
        [(1024, 128)],
        pair, og, ob, owi,
    )
    got = exchange(sent, OUT_GROUP)
    left, right = call(
        split_kernel_out,
        [((256, 256), BF16), ((256, 256), BF16)],
        [(128, 128), (256, 128)],
        got,
    )
    left = lax.all_gather(left, "core", axis=0, tiled=True)
    right = lax.all_gather(right, ("zl", "core"), axis=0, tiled=True)
    (sent,) = call(product_kernel_out, [((512, 128), BF16)], [], left, right)
    got = exchange(sent, OUT_GROUP)
    sent, first, gate = call(
        middle_kernel,
        [((1024, 128), BF16), ((512, CH), BF16), ((512, CH), F32)],
        [(512, 128), (1024, 128)],
        pair, got, gate, omg, omb, owo, ig, ib, iwi,
    )
    got = exchange(sent, IN_GROUP)
    left, right = call(
        split_kernel_in,
        [((128, 512), BF16), ((512, 128), BF16)],
        [(256, 128)],
        got,
    )
    left = lax.all_gather(left, ("xh", "core"), axis=0, tiled=True)
    (sent,) = call(product_kernel_in, [((512, 128), BF16)], [(512, 128)], left, right)
    got = exchange(sent, IN_GROUP)
    (updated,) = call(
        close_kernel,
        [((ROWS, COLS, CH), BF16)],
        [(512, 128)],
        first, got, gate, img, imb, iwo,
    )
    return updated


def solution(mesh):
    fine = Mesh(mesh.devices.reshape(4, 2, 4, 2, 2, 2, 2), AXES)
    return jax.shard_map(
        shards,
        mesh=fine,
        in_specs=(P(ROW, COL, None),) + (P(),) * 12,
        out_specs=P(ROW, COL, None),
        check_vma=False,
    )
```

time: 135 us -> 127 us (0.941)
  blocking collectives: 77.4 us -> 116 us
  starting transfers between devices: 20.8 us -> 0 us
  waiting for transfers between devices: 13.7 us -> 0 us
  local copies, waits for them, and re-layouts: 14.5 us -> 3.83 us
  Pallas kernels: 0 us -> 7.15 us
  other arithmetic: 3.58 us -> 0 us
  matrix products: 3.56 us -> 0 us
    all_to_all x3 -> x4, blocking collectives: 55.3 us -> 92.9 us  [exchange(): lax.all_to_all(values.reshape(128, size, 128), group, 0, 0, tiled=True)]
    all_to_all x1 -> x0, starting transfers between devices: 20.8 us -> none  [exchange(): return lax.all_to_all(values, group, 0, 0, tiled=True)]
    all_to_all x1 -> x0, waiting for transfers between devices: 13.7 us -> none  [exchange(): return lax.all_to_all(values, group, 0, 0, tiled=True)]
    pallas_call x0 -> x7, Pallas kernels: none -> 7.15 us  [call(): pl.pallas_call(kernel, out_shape=outs, in_specs=[whole] * len(operands),...]
    dot_general x6 -> x0, matrix products: 3.56 us -> none  [the longest x2 1.67 us: project_all(): jnp.einsum('ijc,cd->ijd', normed, weight_in, preferred_element_type=jnp.f...]
    reduce_sum x7 -> x0, other arithmetic: 3.21 us -> none  [the longest x4 1.88 us: layer_norm(): spread = jnp.mean(center * center, axis=-1, keepdims=True)]
    unnamed x30 -> x26, local copies, waits for them, and re-layouts: 6.68 us -> 3.83 us
    transpose x4 -> x0, local copies, waits for them, and re-layouts: 2.55 us -> none  [the longest x2 2.24 us: project_all(): return (both.transpose(3, 0, 1, 2), gating)]
  transfers between devices with their start and end apart: 1 -> 0, of which waited for: 1 -> 0; matrix products, arithmetic and copies ran while one was open for 0% -> 0% of each run, Pallas kernels for 0% -> 0%
where the time goes in v3:
time: 127 us
  blocking collectives  116 us (91%)
  Pallas kernels  7.15 us (6%)
  local copies, waits for them, and re-layouts  3.83 us (3%)
    all_to_all x4, blocking collectives, exchange(): lax.all_to_all(values.reshape(128, size, 128), group, 0, 0, tiled=True)  92.9 us
    all_gather x1, blocking collectives, shards(): left = lax.all_gather(left, ('xh', 'core'), axis=0, tiled=True)  11.1 us
    all_gather x1, blocking collectives, shards(): right = lax.all_gather(right, ('zl', 'core'), axis=0, tiled=True)  7.35 us
    pallas_call x7, Pallas kernels, call(): pl.pallas_call(kernel, out_shape=outs, in_specs=[whole] * len(operands),...  7.15 us
    all_gather x1, blocking collectives, shards(): left = lax.all_gather(left, 'core', axis=0, tiled=True)  4.63 us
    unnamed x26, local copies, waits for them, and re-layouts  3.83 us

profile of v3, /device:TPU:1, one launch (start us, length us, event | category | flops | bytes accessed | tf_op | source)
XLA Modules:
  0.0 127.1 jit_solution(4906010809641169419)
XLA Ops:
  0.0 0.0 copy-start.5
  0.0 0.0 copy-start.6
  0.0 0.7 copy-done.5
  0.7 0.0 copy-done.6
  0.7 0.0 copy-start
  0.7 0.9 copy-done
  1.6 0.0 copy-start.2
  1.6 0.9 copy-done.2
  2.5 1.7 %shard_map.127 = (bf16[1024,128]{1,0:T(8,128)(2,1)S(1)}, f32[512,128]{1,0:T(8,128)S(1)}, bf16[512,128]{1,0:T(8,128)(2,1)S(1)}) custom-call(bf16[14,28,128]{2,1,0:T(8,128)(2,1)S(1)} %copy-done.2, f32[1,128]{1,0:T(1,128)S(1)} %bitcast.24, f32[1,128]{1,0:T(1,128)S(1)} %bitcast.25, bf16[128,640]{1,0:T(8,128)(2,1)S(1)} %copy-done), custom_call_target="tpu_custom_call" | custom-call | tf_op jit(solution)/shard_map/pallas_call | solution.py:165
  4.2 35.2 %all_to_all.20 = bf16[128,8,128]{2,1,0:T(8,128)(2,1)S(1)} all-to-all(bf16[128,8,128]{2,1,0:T(8,128)(2,1)S(1)} %bitcast.23), channel_id=1, replica_groups=mesh['zh'=4,'zl'=2,'ylo'=4,'yhi'=2,'xh'=2,'xl'=2,'core'=2] {'yhi','xh','..., dimensions={0} | all-to-all | bytes 524288 | tf_op jit(solution)/shard_map/all_to_all | solution.py:177
  39.4 0.4 shard_map.128
  39.8 4.6 %all_gather.9.left = bf16[512,256]{1,0:T(8,128)(2,1)S(1)} all-gather(bf16[256,256]{1,0:T(8,128)(2,1)S(1)} %get-tuple-element.17), channel_id=1, replica_groups=mesh['zh'=4,'zl'=2,'ylo'=4,'yhi'=2,'xh'=2,'xl'=2,'core'=2] {'core'}, dimensions={0}, use_global_device_ids=true | all-gather | bytes 393216 | tf_op jit(solution)/shard_map/all_gather | solution.py:196
  44.4 7.3 %all_gather.10.right = bf16[1024,256]{1,0:T(8,128)(2,1)S(1)} all-gather(bf16[256,256]{1,0:T(8,128)(2,1)S(1)} %get-tuple-element.18), channel_id=1, replica_groups=mesh['zh'=4,'zl'=2,'ylo'=4,'yhi'=2,'xh'=2,'xl'=2,'core'=2] {'zl','core'}, dimensions={0}, use_global_device_ids=true | all-gather | bytes 655360 | tf_op jit(solution)/shard_map/all_gather | solution.py:197
  51.7 0.5 shard_map.129
  52.2 0.0 copy-start.1
  52.2 0.0 copy-start.3
  52.2 0.0 copy-start.10
  52.2 19.1 %all_to_all.21 = bf16[128,4,128]{2,1,0:T(4,128)(2,1)S(1)} all-to-all(bf16[128,4,128]{2,1,0:T(4,128)(2,1)S(1)} %bitcast.18), channel_id=1, replica_groups=mesh['zh'=4,'zl'=2,'ylo'=4,'yhi'=2,'xh'=2,'xl'=2,'core'=2] {'yhi','xh','..., dimensions={0} | all-to-all | bytes 262144 | tf_op jit(solution)/shard_map/all_to_all | solution.py:177
  71.3 0.0 copy-start.7
  71.3 0.0 copy-start.8
  71.3 0.0 copy-start.9
  71.3 0.0 copy-done.1
  71.3 0.0 copy-done.3
  71.3 0.0 copy-done.10
  71.4 0.6 copy-done.7
  72.0 0.0 copy-done.8
  72.0 0.0 copy-done.9
  72.0 2.4 %shard_map.130 = (bf16[1024,128]{1,0:T(8,128)(2,1)S(1)}, bf16[512,128]{1,0:T(8,128)(2,1)S(1)}, f32[512,128]{1,0:T(8,128)S(1)}) custom-call(bf16[512,128]{1,0:T(8,128)(2,1)S(1)} %get-tuple-element.15.pair, bf16[512,128]{1,0:T(8,128)(2,1)S(1)} %bitcast.19, f32[512,128]{1,0:T(8,128)S(1)} %get-tuple-element.19.gate, f32[1,128]{1,0:T(1,128)S(1)} %bitcast.26, ...), custom_call_target="tpu_custom_call" | custom-call | tf_op jit(solution)/shard_map/pallas_call | solution.py:165
  74.4 19.9 %all_to_all.22 = bf16[128,8,128]{2,1,0:T(8,128)(2,1)S(1)} all-to-all(bf16[128,8,128]{2,1,0:T(8,128)(2,1)S(1)} %bitcast.22), channel_id=1, replica_groups=mesh['zh'=4,'zl'=2,'ylo'=4,'yhi'=2,'xh'=2,'xl'=2,'core'=2] {'yhi','xl','..., dimensions={0} | all-to-all | bytes 524288 | tf_op jit(solution)/shard_map/all_to_all | solution.py:177
  94.3 0.4 shard_map.131
  94.6 11.1 %all_gather.11.left = bf16[512,512]{1,0:T(8,128)(2,1)S(1)} all-gather(bf16[128,512]{1,0:T(8,128)(2,1)S(1)} %get-tuple-element.22), channel_id=1, replica_groups=mesh['zh'=4,'zl'=2,'ylo'=4,'yhi'=2,'xh'=2,'xl'=2,'core'=2] {'xh','core'}, dimensions={0}, use_global_device_ids=true | all-gather | bytes 655360 | tf_op jit(solution)/shard_map/all_gather | solution.py:213
  105.8 0.5 shard_map.132
  106.2 0.0 copy-start.4
  106.3 18.7 %all_to_all.23 = bf16[128,4,128]{2,1,0:T(4,128)(2,1)S(1)} all-to-all(bf16[128,4,128]{2,1,0:T(4,128)(2,1)S(1)} %bitcast.21), channel_id=1, replica_groups=mesh['zh'=4,'zl'=2,'ylo'=4,'yhi'=2,'xh'=2,'xl'=2,'core'=2] {'yhi','xl','..., dimensions={0} | all-to-all | bytes 262144 | tf_op jit(solution)/shard_map/all_to_all | solution.py:177
  125.0 0.0 copy-start.11
  125.0 0.0 copy-start.12
  125.0 0.0 copy-done.4
  125.0 0.6 copy-done.11
  125.6 0.0 copy-done.12
  125.6 1.5 %shard_map.133 = bf16[14,28,128]{2,1,0:T(8,128)(2,1)} custom-call(bf16[512,128]{1,0:T(8,128)(2,1)S(1)} %get-tuple-element.20.first, bf16[512,128]{1,0:T(8,128)(2,1)S(1)} %bitcast.20, f32[512,128]{1,0:T(8,128)S(1)} %get-tuple-element.24.gate, f32[1,128]{1,0:T(1,128)S(1)} %bitcast.30, f32[1,128]{1,0:T(1,128)S(1)} %bitcast.31, bf16[128,128]{1,0:T(8,128)(2,1)S(1)} %copy-done.4), custom_call_target="tpu_custom_call" | custom-call | tf_op jit(solution)/shard_map/pallas_call | solution.py:165
Async XLA Ops:
  0.0 0.7 copy-start.5
  0.0 0.7 copy-start.6
  0.7 0.9 copy-start
  1.6 0.9 copy-start.2
  52.2 19.1 %copy-start.1 = (bf16[128,640]{1,0:T(8,128)(2,1)S(1)}, bf16[128,640]{1,0:T(8,128)(2,1)}, u32[]{:S(2)}) copy-start(bf16[128,640]{1,0:T(8,128)(2,1)} %weight.3) | copy-start | bytes 491524
  52.2 19.1 %copy-start.3 = (bf16[128,128]{1,0:T(8,128)(2,1)S(1)}, bf16[128,128]{1,0:T(8,128)(2,1)}, u32[]{:S(2)}) copy-start(bf16[128,128]{1,0:T(8,128)(2,1)} %weight_out.2) | copy-start | bytes 98308
  52.2 19.1 %copy-start.10 = (f32[128]{0:T(128)S(1)}, f32[128]{0:T(128)}, u32[]{:S(2)}) copy-start(f32[128]{0:T(128)} %param.21) | copy-start | bytes 1540
  71.3 0.7 copy-start.7
  71.3 0.7 copy-start.8
  71.3 0.7 copy-start.9
  106.2 18.7 %copy-start.4 = (bf16[128,128]{1,0:T(8,128)(2,1)S(1)}, bf16[128,128]{1,0:T(8,128)(2,1)}, u32[]{:S(2)}) copy-start(bf16[128,128]{1,0:T(8,128)(2,1)} %weight_out.3) | copy-start | bytes 98308
  125.0 0.7 copy-start.11
  125.0 0.7 copy-start.12

commit v4 on v3

v4 whole, which is shorter than its diff:
```python
import jax
import jax.numpy as jnp
from jax import lax
from jax.experimental import pallas as pl
from jax.experimental.pallas import tpu as pltpu
from jax.sharding import Mesh, PartitionSpec as P

CH = 128
EPSILON = 1e-05
ROWS, COLS = 14, 28
F32, BF16 = jnp.float32, jnp.bfloat16

AXES = ("z2", "z1", "z0", "yb", "ya", "yc", "x1", "x0", "core")
ROW, COL = AXES[:5], AXES[5:]
GROUP = ("yc", "yb", "ya", "z2", "z1", "z0", "x0")
SUM_GROUP = ("x1",) + GROUP


NT = (((1,), (1,)), ((), ()))
TN = (((0,), (1,)), ((), ()))


def dot(a, b, dims=(((1,), (0,)), ((), ()))):
    return lax.dot_general(a, b, dims, preferred_element_type=F32)


def iota(shape, axis):
    return lax.broadcasted_iota(jnp.int32, shape, axis)


def residue_of_slot(slot):
    inner = slot % 16
    residue = inner % 4 * 4 + inner // 4
    return jnp.where(residue < ROWS, slot // 16 * ROWS + residue, -1)


def transpose_groups(blocks):
    lane = iota(blocks[0].shape, 1)
    low, even = lane < 64, lane // 32 % 2 == 0
    a, b, c, d = blocks
    a, c = jnp.where(low, a, pltpu.roll(c, 64, 1)), jnp.where(low, pltpu.roll(a, 64, 1), c)
    b, d = jnp.where(low, b, pltpu.roll(d, 64, 1)), jnp.where(low, pltpu.roll(b, 64, 1), d)
    a, b = jnp.where(even, a, pltpu.roll(b, 32, 1)), jnp.where(even, pltpu.roll(a, 96, 1), b)
    c, d = jnp.where(even, c, pltpu.roll(d, 32, 1)), jnp.where(even, pltpu.roll(c, 96, 1), d)
    return [a, b, c, d]


def bits(names, number):
    return {name: number >> (len(names) - 1 - n) & 1 for n, name in enumerate(names)}


def place_in(names, values):
    place = 0
    for name in names:
        place = 2 * place + values[name]
    return place


def gather_blocks(got):
    values = got[...].astype(F32)
    blocks = []
    for c in range(4):
        places = [place_in(GROUP, {**bits(ROW, r), **bits(("yc", "x0"), c)}) for r in range(32)]
        blocks.append(jnp.concatenate([values[8 * p : 8 * (p + 1)] for p in places], axis=0))
    return transpose_groups(blocks)


def scatter_block(block, stage, group, row_names, col_bits):
    for n in range(block.shape[0] // 4):
        place = place_in(group, {**bits(row_names, n), **col_bits})
        stage[4 * place : 4 * (place + 1), :] = block[4 * n : 4 * (n + 1)]


def layer_norm(values, gain, bias):
    center = values - jnp.mean(values, axis=-1, keepdims=True)
    spread = jnp.mean(center * center, axis=-1, keepdims=True)
    return center * lax.rsqrt(spread + EPSILON) * gain + bias


def project(q, values, gain, bias, weight, stage, gate):
    normed = layer_norm(values, gain, bias).astype(BF16)
    lane = iota((CH, 128), 1)
    valid = (lane // 32 * 4 + q < ROWS) & (residue_of_slot(lane % 32) >= 0)
    for side in range(2):
        opened = dot(weight[:, 2 * side * CH : (2 * side + 1) * CH], normed, TN)
        value = dot(weight[:, (2 * side + 1) * CH : (2 * side + 2) * CH], normed, TN)
        operand = jnp.where(valid, jax.nn.sigmoid(opened) * value, 0.0)
        stage[pl.ds(2 * q + side, CH, stride=8), :] = operand
    gate[128 * q : 128 * (q + 1), :] = jax.nn.sigmoid(dot(normed, weight[:, 4 * CH :]))


def finish(q, pair, mixed, gate, gain, bias, weight):
    values = mixed[pl.ds(q, CH, stride=4), :].T
    normed = layer_norm(values, gain, bias).astype(BF16)
    rows = slice(128 * q, 128 * (q + 1))
    return (pair[rows, :].astype(F32) + gate[rows, :] * dot(normed, weight[...])).astype(BF16)


def open_kernel(*refs):
    pair_in, weight_in, params = refs[0], refs[1], refs[2:10]
    sent, gate, spread, vectors, pair, weight, stage, sems = refs[10:]
    copies = [
        pltpu.make_async_copy(pair_in, pair, sems.at[8]),
        pltpu.make_async_copy(weight_in, weight, sems.at[9]),
    ]
    copies += [
        pltpu.make_async_copy(param, vectors.at[pl.ds(n, 1), :], sems.at[n])
        for n, param in enumerate(params)
    ]
    for copy in copies:
        copy.start()
    for copy in copies:
        copy.wait()
    place = (residue_of_slot(iota((32, COLS), 0)) == iota((32, COLS), 1)).astype(BF16)
    for q in range(4):
        parts = [
            dot(place, pair[4 * g + q]) if 4 * g + q < ROWS else jnp.zeros((32, CH), F32)
            for g in range(4)
        ]
        values = jnp.concatenate(parts, axis=0)
        spread[128 * q : 128 * (q + 1), :] = values.astype(BF16)
        project(q, values, vectors[0:1, :], vectors[1:2, :], weight, stage, gate)
    sent[...] = stage[...].astype(BF16)


def middle_kernel(pair, got, gate, vectors, weight_out, weight, sent, first, gate_in, mixed, stage):
    mixed[...] = got[:512, :].astype(F32) + got[512:, :].astype(F32)
    for q in range(4):
        values = finish(q, pair, mixed, gate, vectors[2:3, :], vectors[3:4, :], weight_out)
        first[128 * q : 128 * (q + 1), :] = values
        project(q, values.astype(F32), vectors[4:5, :], vectors[5:6, :], weight, stage, gate_in)
    sent[...] = stage[...].astype(BF16)


def close_kernel(first, got, gate, vectors, weight_out, updated, mixed):
    mixed[...] = got[...].astype(F32)
    place = (residue_of_slot(iota((COLS, 32), 1)) == iota((COLS, 32), 0)).astype(BF16)
    for q in range(4):
        values = finish(q, first, mixed, gate, vectors[6:7, :], vectors[7:8, :], weight_out)
        for g in range(4):
            if 4 * g + q < ROWS:
                updated[4 * g + q] = dot(place, values[32 * g : 32 * (g + 1)]).astype(BF16)


def split_kernel_out(got, both, stage, order):
    for g, block in enumerate(gather_blocks(got)):
        stage[...] = block
        both[128 * g : 128 * (g + 1), :] = stage[pl.ds(0, 128, stride=2), :].astype(BF16)
        order[pl.ds(g, 128, stride=4), :] = stage[pl.ds(1, 128, stride=2), :]
    for c in range(16):
        target = 512 + 32 * (c % 2 * 8 + c // 2)
        both[target : target + 32, :] = order[32 * c : 32 * (c + 1), :].astype(BF16)


def product_kernel_out(both, sent, stage):
    core = lax.axis_index("core")
    mixed = jnp.zeros((512, 256), F32)
    for part in range(2):
        start = pl.multiple_of(1024 * part + 512 + 256 * core, 256)
        mixed += dot(both[1024 * part : 1024 * part + 512, :], both[pl.ds(start, 256), :], NT)
    for yc in range(2):
        blocks = [mixed[128 * g : 128 * (g + 1), 128 * yc : 128 * (yc + 1)] for g in range(4)]
        for c, block in enumerate(transpose_groups(blocks)):
            scatter_block(block, stage, SUM_GROUP, ROW, {"yc": yc, **bits(("x1", "x0"), c)})
    sent[...] = stage[...].astype(BF16)


def split_kernel_in(got, left, right, stage):
    for g, block in enumerate(gather_blocks(got)):
        stage[...] = block
        rows = slice(128 * g, 128 * (g + 1))
        left[:, rows] = stage[pl.ds(0, 128, stride=2), :].T.astype(BF16)
        right[rows, :] = stage[pl.ds(1, 128, stride=2), :].astype(BF16)


def product_kernel_in(left, right, sent, stage, packed):
    stage[...] = dot(left[...], right[...])
    blocks = [stage[pl.ds(g, 128, stride=4), :] for g in range(4)]
    for c, block in enumerate(transpose_groups(blocks)):
        scatter_block(block, packed, GROUP, ("z1", "yb", "z2", "z0", "ya"), bits(("yc", "x0"), c))
    sent[...] = packed[...].astype(BF16)


def call(kernel, outs, scratch, *operands, hbm=False):
    whole = pl.BlockSpec(memory_space=pltpu.VMEM)
    outs = [jax.ShapeDtypeStruct(shape, kind) for shape, kind in outs]
    return pl.pallas_call(
        kernel,
        out_shape=outs,
        in_specs=[pl.BlockSpec(memory_space=pltpu.HBM) if hbm else whole] * len(operands),
        out_specs=[whole] * len(outs),
        scratch_shapes=[pltpu.VMEM(s, F32) if isinstance(s, tuple) else s for s in scratch],
        compiler_params=pltpu.CompilerParams(vmem_limit_bytes=32 * 1024 * 1024),
    )(*operands)


def exchange(values, group, size):
    got = lax.all_to_all(values.reshape(-1, size, 128), group, 0, 0, tiled=True)
    return got.reshape(values.shape)


def shards(pair, og, ob, owi, omg, omb, owo, ig, ib, iwi, img, imb, iwo):
    params = [v.reshape(1, CH) for v in (og, ob, omg, omb, ig, ib, img, imb)]
    sent, gate, pair, vectors = call(
        open_kernel,
        [((1024, 128), BF16), ((512, CH), F32), ((512, CH), BF16), ((8, CH), F32)],
        [
            pltpu.VMEM(pair.shape, BF16),
            pltpu.VMEM(owi.shape, BF16),
            (1024, 128),
            pltpu.SemaphoreType.DMA((10,)),
        ],
        pair, owi, *params,
        hbm=True,
    )
    got = exchange(sent, GROUP, 8)
    (both,) = call(split_kernel_out, [((1024, 128), BF16)], [(256, 128), (512, 128)], got)
    both = lax.all_gather(both, "core", axis=0, tiled=True)
    (sent,) = call(product_kernel_out, [((1024, 128), BF16)], [(1024, 128)], both)
    got = exchange(sent, SUM_GROUP, 4)
    sent, first, gate = call(
        middle_kernel,
        [((1024, 128), BF16), ((512, CH), BF16), ((512, CH), F32)],
        [(512, 128), (1024, 128)],
        pair, got, gate, vectors, owo, iwi,
    )
    got = exchange(sent, GROUP, 8)
    left, right = call(
        split_kernel_in,
        [((128, 512), BF16), ((512, 128), BF16)],
        [(256, 128)],
        got,
    )
    left = lax.all_gather(left, ("x1", "core"), axis=0, tiled=True)
    (sent,) = call(
        product_kernel_in, [((512, 128), BF16)], [(512, 128), (512, 128)], left, right
    )
    got = exchange(sent, GROUP, 4)
    (updated,) = call(
        close_kernel,
        [((ROWS, COLS, CH), BF16)],
        [(512, 128)],
        first, got, gate, vectors, iwo,
    )
    return updated


def solution(mesh):
    fine = Mesh(mesh.devices.reshape((2,) * 9), AXES)
    return jax.shard_map(
        shards,
        mesh=fine,
        in_specs=(P(ROW, COL, None),) + (P(),) * 12,
        out_specs=P(ROW, COL, None),
        check_vma=False,
    )
```

time: 127 us -> 119 us (0.937)
  blocking collectives: 116 us -> 108 us
  local copies, waits for them, and re-layouts: 3.83 us -> 2.55 us
    all_gather x3 -> x2, blocking collectives: 23.1 us -> 16.4 us  [the longest x1 11.6 us: shards(): left = lax.all_gather(left, ('x1', 'core'), axis=0, tiled=True)]
    all_to_all x4, blocking collectives: 92.9 us -> 91.3 us  [exchange(): got = lax.all_to_all(values.reshape(-1, size, 128), group, 0, 0, tiled=True)]
    unnamed x26, local copies, waits for them, and re-layouts: 3.83 us -> 2.55 us
where the time goes in v4:
time: 119 us; the launch traced here: 118 us
  blocking collectives  108 us (91%)
  Pallas kernels  7.7 us (6%)
  local copies, waits for them, and re-layouts  2.55 us (2%)
    all_to_all x4, blocking collectives, exchange(): got = lax.all_to_all(values.reshape(-1, size, 128), group, 0, 0, tiled=True)  91.3 us
    all_gather x1, blocking collectives, shards(): left = lax.all_gather(left, ('x1', 'core'), axis=0, tiled=True)  11.6 us
    pallas_call x7, Pallas kernels, call(): pl.pallas_call(kernel, out_shape=outs, in_specs=[pl.BlockSpec(memory_spac...  7.7 us
    all_gather x1, blocking collectives, shards(): both = lax.all_gather(both, 'core', axis=0, tiled=True)  4.86 us
    unnamed x26, local copies, waits for them, and re-layouts  2.55 us

profile of v4, /device:TPU:1, one launch (start us, length us, event | category | flops | bytes accessed | tf_op | source)
XLA Modules:
  0.0 118.1 jit_solution(15556494765239236158)
XLA Ops:
  0.0 0.0 copy-start.12
  0.0 0.0 copy-start.8
  0.0 0.0 copy-start.9
  0.0 0.0 copy-start.10
  0.0 0.0 copy-start.11
  0.0 0.0 copy-start.5
  0.0 0.0 copy-start.6
  0.0 0.0 copy-start.7
  0.1 0.6 copy-done.12
  0.7 0.0 copy-done.8
  0.7 0.0 copy-done.9
  0.7 0.0 copy-done.10
  0.7 0.0 copy-done.11
  0.7 0.0 copy-done.5
  0.7 0.0 copy-done.6
  0.8 0.0 copy-done.7
  0.8 0.0 copy-start
  0.8 0.9 copy-done
  1.7 0.0 copy-start.2
  1.7 0.9 copy-done.2
  2.6 2.1 %shard_map.127 = (bf16[1024,128]{1,0:T(8,128)(2,1)S(1)}, f32[512,128]{1,0:T(8,128)S(1)}, bf16[512,128]{1,0:T(8,128)(2,1)S(1)}, f32[8,128]{1,0:T(8,128)S(1)}) custom-call(bf16[14,28,128]{2,1,0:T(8,128)(2,1)S(1)} %copy-done.2, bf16[128,640]{1,0:T(8,128)(2,1)S(1)} %copy-done, f32[1,128]{1,0:T(1,128)S(1)} %bitcast.24, f32[1,128]{1,0:T(1,128)S(1)} %bitcast.25, ...), custom_call_target="tpu_custom_call" | custom-call | tf_op jit(solution)/shard_map/pallas_call | solution.py:187
  4.7 31.9 %all_to_all.20 = bf16[128,8,128]{2,1,0:T(8,128)(2,1)S(1)} all-to-all(bf16[128,8,128]{2,1,0:T(8,128)(2,1)S(1)} %bitcast.23), channel_id=1, replica_groups=mesh['z2'=2,'z1'=2,'z0'=2,'yb'=2,'ya'=2,'yc'=2,'x1'=2,'x0'=2,'core'=2] {..., dimensions={0} | all-to-all | bytes 524288 | tf_op jit(solution)/shard_map/all_to_all | solution.py:198
  36.6 0.3 shard_map.128
  36.9 4.9 %all_gather.6.both = bf16[2048,128]{1,0:T(8,128)(2,1)S(1)} all-gather(bf16[1024,128]{1,0:T(8,128)(2,1)S(1)} %shard_map.128), channel_id=1, replica_groups=mesh['z2'=2,'z1'=2,'z0'=2,'yb'=2,'ya'=2,'yc'=2,'x1'=2,'x0'=2,'core'=2] {..., dimensions={0}, use_global_device_ids=true | all-gather | bytes 786432 | tf_op jit(solution)/shard_map/all_gather | solution.py:218
  41.7 0.6 shard_map.129
  42.3 0.0 copy-start.1
  42.3 0.0 copy-start.3
  42.3 24.2 %all_to_all.21 = bf16[256,4,128]{2,1,0:T(4,128)(2,1)S(1)} all-to-all(bf16[256,4,128]{2,1,0:T(4,128)(2,1)S(1)} %bitcast.16), channel_id=1, replica_groups=mesh['z2'=2,'z1'=2,'z0'=2,'yb'=2,'ya'=2,'yc'=2,'x1'=2,'x0'=2,'core'=2] {..., dimensions={0} | all-to-all | bytes 524288 | tf_op jit(solution)/shard_map/all_to_all | solution.py:198
  66.5 0.0 copy-done.1
  66.5 0.0 copy-done.3
  66.5 2.4 %shard_map.130 = (bf16[1024,128]{1,0:T(8,128)(2,1)S(1)}, bf16[512,128]{1,0:T(8,128)(2,1)S(1)}, f32[512,128]{1,0:T(8,128)S(1)}) custom-call(bf16[512,128]{1,0:T(8,128)(2,1)S(1)} %get-tuple-element.14.pair, bf16[1024,128]{1,0:T(8,128)(2,1)S(1)} %bitcast.17, f32[512,128]{1,0:T(8,128)S(1)} %get-tuple-element.16.gate, f32[8,128]{1,0:T(8,128)S(1)} %get-tuple-element.17.vectors, ...), custom_call_target="tpu_custom_call" | custom-call | tf_op jit(solution)/shard_map/pallas_call | solution.py:187
  68.9 18.0 %all_to_all.22 = bf16[128,8,128]{2,1,0:T(8,128)(2,1)S(1)} all-to-all(bf16[128,8,128]{2,1,0:T(8,128)(2,1)S(1)} %bitcast.22), channel_id=1, replica_groups=mesh['z2'=2,'z1'=2,'z0'=2,'yb'=2,'ya'=2,'yc'=2,'x1'=2,'x0'=2,'core'=2] {..., dimensions={0} | all-to-all | bytes 524288 | tf_op jit(solution)/shard_map/all_to_all | solution.py:198
  86.9 0.4 shard_map.131
  87.3 11.6 %all_gather.7.left = bf16[512,512]{1,0:T(8,128)(2,1)S(1)} all-gather(bf16[128,512]{1,0:T(8,128)(2,1)S(1)} %get-tuple-element.20), channel_id=1, replica_groups=mesh['z2'=2,'z1'=2,'z0'=2,'yb'=2,'ya'=2,'yc'=2,'x1'=2,'x0'=2,'core'=2] {..., dimensions={0}, use_global_device_ids=true | all-gather | bytes 655360 | tf_op jit(solution)/shard_map/all_gather | solution.py:234
  98.8 0.5 shard_map.132
  99.4 0.0 copy-start.4
  99.4 17.3 %all_to_all.23 = bf16[128,4,128]{2,1,0:T(4,128)(2,1)S(1)} all-to-all(bf16[128,4,128]{2,1,0:T(4,128)(2,1)S(1)} %bitcast.21), channel_id=1, replica_groups=mesh['z2'=2,'z1'=2,'z0'=2,'yb'=2,'ya'=2,'yc'=2,'x1'=2,'x0'=2,'core'=2] {..., dimensions={0} | all-to-all | bytes 262144 | tf_op jit(solution)/shard_map/all_to_all | solution.py:198
  116.7 0.0 copy-done.4
  116.7 1.5 %shard_map.133 = bf16[14,28,128]{2,1,0:T(8,128)(2,1)} custom-call(bf16[512,128]{1,0:T(8,128)(2,1)S(1)} %get-tuple-element.18.first, bf16[512,128]{1,0:T(8,128)(2,1)S(1)} %bitcast.20, f32[512,128]{1,0:T(8,128)S(1)} %get-tuple-element.22.gate, f32[8,128]{1,0:T(8,128)S(1)} %get-tuple-element.17.vectors, bf16[128,128]{1,0:T(8,128)(2,1)S(1)} %copy-done.4), custom_call_target="tpu_custom_call" | custom-call | tf_op jit(solution)/shard_map/pallas_call | solution.py:187
Async XLA Ops:
  0.0 0.7 copy-start.12
  0.0 0.7 copy-start.8
  0.0 0.7 copy-start.9
  0.0 0.7 copy-start.10
  0.0 0.7 copy-start.11
  0.0 0.7 copy-start.5
  0.0 0.7 copy-start.6
  0.0 0.7 copy-start.7
  0.8 0.9 copy-start
  1.7 0.9 copy-start.2
  42.3 24.2 %copy-start.1 = (bf16[128,640]{1,0:T(8,128)(2,1)S(1)}, bf16[128,640]{1,0:T(8,128)(2,1)}, u32[]{:S(2)}) copy-start(bf16[128,640]{1,0:T(8,128)(2,1)} %weight.1) | copy-start | bytes 491524
  42.3 24.2 %copy-start.3 = (bf16[128,128]{1,0:T(8,128)(2,1)S(1)}, bf16[128,128]{1,0:T(8,128)(2,1)}, u32[]{:S(2)}) copy-start(bf16[128,128]{1,0:T(8,128)(2,1)} %weight_out.2) | copy-start | bytes 98308
  99.4 17.3 %copy-start.4 = (bf16[128,128]{1,0:T(8,128)(2,1)S(1)}, bf16[128,128]{1,0:T(8,128)(2,1)}, u32[]{:S(2)}) copy-start(bf16[128,128]{1,0:T(8,128)(2,1)} %weight_out.3) | copy-start | bytes 98308

commit v5 on v4

--- a/solution.py
+++ b/solution.py
@@ -12,12 +12,11 @@
 
 AXES = ("z2", "z1", "z0", "yb", "ya", "yc", "x1", "x0", "core")
 ROW, COL = AXES[:5], AXES[5:]
-GROUP = ("yc", "yb", "ya", "z2", "z1", "z0", "x0")
-SUM_GROUP = ("x1",) + GROUP
+GROUP = ("yc", "yb", "ya", "z0", "z1", "z2", "x0")
+SUM_GROUP = GROUP + ("x1",)
 
 
 NT = (((1,), (1,)), ((), ()))
-TN = (((0,), (1,)), ((), ()))
 
 
 def dot(a, b, dims=(((1,), (0,)), ((), ()))):
@@ -72,74 +71,93 @@
 
 
 def layer_norm(values, gain, bias):
-    center = values - jnp.mean(values, axis=-1, keepdims=True)
-    spread = jnp.mean(center * center, axis=-1, keepdims=True)
+    center = values - jnp.mean(values, axis=0, keepdims=True)
+    spread = jnp.mean(center * center, axis=0, keepdims=True)
     return center * lax.rsqrt(spread + EPSILON) * gain + bias
+
+
+def columns(vectors, *rows):
+    turned = vectors.T
+    return [jnp.broadcast_to(turned[:, row : row + 1], (CH, 128)) for row in rows]
 
 
 def project(q, values, gain, bias, weight, stage, gate):
     normed = layer_norm(values, gain, bias).astype(BF16)
+    projected = dot(weight, normed)
     lane = iota((CH, 128), 1)
     valid = (lane // 32 * 4 + q < ROWS) & (residue_of_slot(lane % 32) >= 0)
     for side in range(2):
-        opened = dot(weight[:, 2 * side * CH : (2 * side + 1) * CH], normed, TN)
-        value = dot(weight[:, (2 * side + 1) * CH : (2 * side + 2) * CH], normed, TN)
+        opened = projected[2 * side * CH : (2 * side + 1) * CH]
+        value = projected[(2 * side + 1) * CH : (2 * side + 2) * CH]
         operand = jnp.where(valid, jax.nn.sigmoid(opened) * value, 0.0)
         stage[pl.ds(2 * q + side, CH, stride=8), :] = operand
-    gate[128 * q : 128 * (q + 1), :] = jax.nn.sigmoid(dot(normed, weight[:, 4 * CH :]))
+    gate[:CH, 128 * q : 128 * (q + 1)] = jax.nn.sigmoid(projected[4 * CH :])
 
 
 def finish(q, pair, mixed, gate, gain, bias, weight):
-    values = mixed[pl.ds(q, CH, stride=4), :].T
-    normed = layer_norm(values, gain, bias).astype(BF16)
-    rows = slice(128 * q, 128 * (q + 1))
-    return (pair[rows, :].astype(F32) + gate[rows, :] * dot(normed, weight[...])).astype(BF16)
+    normed = layer_norm(mixed, gain, bias).astype(BF16)
+    lanes = slice(128 * q, 128 * (q + 1))
+    return (pair[:, lanes].astype(F32) + gate[:CH, lanes] * dot(weight, normed)).astype(BF16)
 
 
 def open_kernel(*refs):
     pair_in, weight_in, params = refs[0], refs[1], refs[2:10]
-    sent, gate, spread, vectors, pair, weight, stage, sems = refs[10:]
-    copies = [
-        pltpu.make_async_copy(pair_in, pair, sems.at[8]),
-        pltpu.make_async_copy(weight_in, weight, sems.at[9]),
-    ]
+    sent, gate, spread, pair, weight, stage, sems = refs[10:]
+    pair_copy = pltpu.make_async_copy(pair_in, pair, sems.at[8])
+    copies = [pltpu.make_async_copy(weight_in, weight, sems.at[9])]
     copies += [
-        pltpu.make_async_copy(param, vectors.at[pl.ds(n, 1), :], sems.at[n])
+        pltpu.make_async_copy(param, gate.at[pl.ds(CH + n, 1), pl.ds(0, CH)], sems.at[n])
         for n, param in enumerate(params)
     ]
-    for copy in copies:
+    for copy in [pair_copy, *copies]:
         copy.start()
-    for copy in copies:
-        copy.wait()
+    pair_copy.wait()
     place = (residue_of_slot(iota((32, COLS), 0)) == iota((32, COLS), 1)).astype(BF16)
+    values = []
     for q in range(4):
         parts = [
             dot(place, pair[4 * g + q]) if 4 * g + q < ROWS else jnp.zeros((32, CH), F32)
             for g in range(4)
         ]
-        values = jnp.concatenate(parts, axis=0)
-        spread[128 * q : 128 * (q + 1), :] = values.astype(BF16)
-        project(q, values, vectors[0:1, :], vectors[1:2, :], weight, stage, gate)
+        values.append(jnp.concatenate(parts, axis=0).T)
+        spread[:, 128 * q : 128 * (q + 1)] = values[q].astype(BF16)
+    for copy in copies:
+        copy.wait()
+    gain, bias = columns(gate[CH:, :CH], 0, 1)
+    turned = weight[...].T
+    for q in range(4):
+        project(q, values[q], gain, bias, turned, stage, gate)
     sent[...] = stage[...].astype(BF16)
 
 
-def middle_kernel(pair, got, gate, vectors, weight_out, weight, sent, first, gate_in, mixed, stage):
-    mixed[...] = got[:512, :].astype(F32) + got[512:, :].astype(F32)
-    for q in range(4):
-        values = finish(q, pair, mixed, gate, vectors[2:3, :], vectors[3:4, :], weight_out)
-        first[128 * q : 128 * (q + 1), :] = values
-        project(q, values.astype(F32), vectors[4:5, :], vectors[5:6, :], weight, stage, gate_in)
+def middle_kernel(pair, got, gate, weight_out, weight, sent, first, gate_in, mixed, stage):
+    mixed[...] = got[...].astype(F32)
+    vectors = gate[CH:, :CH]
+    gate_in[CH:, :CH] = vectors
+    mix_gain, mix_bias, gain, bias = columns(vectors, 2, 3, 4, 5)
+    turned_out, turned = weight_out[...].T, weight[...].T
+    for q in range(4):
+        values = mixed[pl.ds(q, CH, stride=8), :] + mixed[pl.ds(4 + q, CH, stride=8), :]
+        values = finish(q, pair, values, gate, mix_gain, mix_bias, turned_out)
+        first[:, 128 * q : 128 * (q + 1)] = values
+        project(q, values.astype(F32), gain, bias, turned, stage, gate_in)
     sent[...] = stage[...].astype(BF16)
 
 
-def close_kernel(first, got, gate, vectors, weight_out, updated, mixed):
+def close_kernel(first, got, gate, weight_out, updated, mixed):
     mixed[...] = got[...].astype(F32)
-    place = (residue_of_slot(iota((COLS, 32), 1)) == iota((COLS, 32), 0)).astype(BF16)
-    for q in range(4):
-        values = finish(q, first, mixed, gate, vectors[6:7, :], vectors[7:8, :], weight_out)
+    gain, bias = columns(gate[CH:, :CH], 6, 7)
+    turned = weight_out[...].T
+    row, lane = iota((128, 128), 0), iota((128, 128), 1)
+    place = (row // 32 == lane // 32) & (residue_of_slot(lane % 32) == row % 32)
+    place = place.astype(F32).astype(BF16)
+    for q in range(4):
+        values = mixed[pl.ds(q, CH, stride=4), :]
+        values = finish(q, first, values, gate, gain, bias, turned)
+        values = dot(place, values, NT).astype(BF16)
         for g in range(4):
             if 4 * g + q < ROWS:
-                updated[4 * g + q] = dot(place, values[32 * g : 32 * (g + 1)]).astype(BF16)
+                updated[4 * g + q] = values[32 * g : 32 * g + COLS]
 
 
 def split_kernel_out(got, both, stage, order):
@@ -190,7 +208,7 @@
         in_specs=[pl.BlockSpec(memory_space=pltpu.HBM) if hbm else whole] * len(operands),
         out_specs=[whole] * len(outs),
         scratch_shapes=[pltpu.VMEM(s, F32) if isinstance(s, tuple) else s for s in scratch],
-        compiler_params=pltpu.CompilerParams(vmem_limit_bytes=32 * 1024 * 1024),
+        compiler_params=pltpu.CompilerParams(vmem_limit_bytes=(62 if hbm else 32) * 1024 * 1024),
     )(*operands)
 
 
@@ -201,9 +219,9 @@
 
 def shards(pair, og, ob, owi, omg, omb, owo, ig, ib, iwi, img, imb, iwo):
     params = [v.reshape(1, CH) for v in (og, ob, omg, omb, ig, ib, img, imb)]
-    sent, gate, pair, vectors = call(
+    sent, gate, pair = call(
         open_kernel,
-        [((1024, 128), BF16), ((512, CH), F32), ((512, CH), BF16), ((8, CH), F32)],
+        [((1024, 128), BF16), ((CH + 8, 512), F32), ((CH, 512), BF16)],
         [
             pltpu.VMEM(pair.shape, BF16),
             pltpu.VMEM(owi.shape, BF16),
@@ -220,9 +238,9 @@
     got = exchange(sent, SUM_GROUP, 4)
     sent, first, gate = call(
         middle_kernel,
-        [((1024, 128), BF16), ((512, CH), BF16), ((512, CH), F32)],
-        [(512, 128), (1024, 128)],
-        pair, got, gate, vectors, owo, iwi,
+        [((1024, 128), BF16), ((CH, 512), BF16), ((CH + 8, 512), F32)],
+        [(1024, 128), (1024, 128)],
+        pair, got, gate, owo, iwi,
     )
     got = exchange(sent, GROUP, 8)
     left, right = call(
@@ -240,7 +258,7 @@
         close_kernel,
         [((ROWS, COLS, CH), BF16)],
         [(512, 128)],
-        first, got, gate, vectors, iwo,
+        first, got, gate, iwo,
     )
     return updated
 

time: 119 us -> 114 us (0.958)
  local copies, waits for them, and re-layouts: 2.55 us -> 0.03 us
    unnamed x26 -> x10, local copies, waits for them, and re-layouts: 2.55 us -> 0.03 us
where the time goes in v5:
time: 114 us
  blocking collectives  107 us (94%)
  Pallas kernels  6.74 us (6%)
    all_to_all x4, blocking collectives, exchange(): got = lax.all_to_all(values.reshape(-1, size, 128), group, 0, 0, tiled=True)  90.7 us
    all_gather x1, blocking collectives, shards(): left = lax.all_gather(left, ('x1', 'core'), axis=0, tiled=True)  11.6 us
    pallas_call x7, Pallas kernels, call(): pl.pallas_call(kernel, out_shape=outs, in_specs=[pl.BlockSpec(memory_spac...  6.74 us
    all_gather x1, blocking collectives, shards(): both = lax.all_gather(both, 'core', axis=0, tiled=True)  4.86 us

profile of v5, /device:TPU:1, one launch (start us, length us, event | category | flops | bytes accessed | tf_op | source)
XLA Modules:
  0.0 114.0 jit_solution(535335015874295787)
XLA Ops:
  0.0 2.7 %shard_map.127 = (bf16[1024,128]{1,0:T(8,128)(2,1)}, f32[136,512]{1,0:T(8,128)}, bf16[128,512]{1,0:T(8,128)(2,1)}) custom-call(bf16[14,28,128]{2,1,0:T(8,128)(2,1)} %refs_0_.1, bf16[128,640]{1,0:T(8,128)(2,1)} %refs_1_.1, f32[1,128]{1,0:T(1,128)} %bitcast.24, f32[1,128]{1,0:T(1,128)} %bitcast.25, f32[1,128]{1,0:T(1,128)} %bitcast.26, f32[1,128]{1,0:T(1,128)} %bitcast.27, ...), custom_call_target="tpu_custom_call" | custom-call | tf_op jit(solution)/shard_map/pallas_call | solution.py:205
  2.7 32.1 %all_to_all.20 = bf16[128,8,128]{2,1,0:T(8,128)(2,1)S(1)} all-to-all(bf16[128,8,128]{2,1,0:T(8,128)(2,1)} %bitcast.23), channel_id=1, replica_groups=mesh['z2'=2,'z1'=2,'z0'=2,'yb'=2,'ya'=2,'yc'=2,'x1'=2,'x0'=2,'core'=2] {..., dimensions={0} | all-to-all | bytes 524288 | tf_op jit(solution)/shard_map/all_to_all | solution.py:216
  34.8 0.3 shard_map.128
  35.1 4.9 %all_gather.6.both = bf16[2048,128]{1,0:T(8,128)(2,1)S(1)} all-gather(bf16[1024,128]{1,0:T(8,128)(2,1)S(1)} %shard_map.128), channel_id=1, replica_groups=mesh['z2'=2,'z1'=2,'z0'=2,'yb'=2,'ya'=2,'yc'=2,'x1'=2,'x0'=2,'core'=2] {..., dimensions={0}, use_global_device_ids=true | all-gather | bytes 786432 | tf_op jit(solution)/shard_map/all_gather | solution.py:236
  39.9 0.0 copy-start.2
  39.9 0.5 shard_map.129
  40.5 0.0 copy-start
  40.5 0.0 copy-start.1
  40.5 0.0 copy-start.3
  40.5 23.5 %all_to_all.21 = bf16[256,4,128]{2,1,0:T(4,128)(2,1)S(1)} all-to-all(bf16[256,4,128]{2,1,0:T(4,128)(2,1)S(1)} %bitcast.16), channel_id=1, replica_groups=mesh['z2'=2,'z1'=2,'z0'=2,'yb'=2,'ya'=2,'yc'=2,'x1'=2,'x0'=2,'core'=2] {..., dimensions={0} | all-to-all | bytes 524288 | tf_op jit(solution)/shard_map/all_to_all | solution.py:216
  64.0 0.0 copy-done.2
  64.0 0.0 copy-done
  64.0 0.0 copy-done.1
  64.0 0.0 copy-done.3
  64.1 1.0 shard_map.130
  65.1 18.1 %all_to_all.22 = bf16[128,8,128]{2,1,0:T(8,128)(2,1)S(1)} all-to-all(bf16[128,8,128]{2,1,0:T(8,128)(2,1)S(1)} %bitcast.22), channel_id=1, replica_groups=mesh['z2'=2,'z1'=2,'z0'=2,'yb'=2,'ya'=2,'yc'=2,'x1'=2,'x0'=2,'core'=2] {..., dimensions={0} | all-to-all | bytes 524288 | tf_op jit(solution)/shard_map/all_to_all | solution.py:216
  83.2 0.4 shard_map.131
  83.5 11.6 %all_gather.7.left = bf16[512,512]{1,0:T(8,128)(2,1)S(1)} all-gather(bf16[128,512]{1,0:T(8,128)(2,1)S(1)} %get-tuple-element.18), channel_id=1, replica_groups=mesh['z2'=2,'z1'=2,'z0'=2,'yb'=2,'ya'=2,'yc'=2,'x1'=2,'x0'=2,'core'=2] {..., dimensions={0}, use_global_device_ids=true | all-gather | bytes 655360 | tf_op jit(solution)/shard_map/all_gather | solution.py:252
  95.2 0.5 shard_map.132
  95.7 0.0 copy-start.4
  95.7 17.0 %all_to_all.23 = bf16[128,4,128]{2,1,0:T(4,128)(2,1)S(1)} all-to-all(bf16[128,4,128]{2,1,0:T(4,128)(2,1)S(1)} %bitcast.21), channel_id=1, replica_groups=mesh['z2'=2,'z1'=2,'z0'=2,'yb'=2,'ya'=2,'yc'=2,'x1'=2,'x0'=2,'core'=2] {..., dimensions={0} | all-to-all | bytes 262144 | tf_op jit(solution)/shard_map/all_to_all | solution.py:216
  112.7 0.0 copy-done.4
  112.7 1.3 %shard_map.133 = bf16[14,28,128]{2,1,0:T(8,128)(2,1)} custom-call(bf16[128,512]{1,0:T(8,128)(2,1)S(1)} %get-tuple-element.16.first, bf16[512,128]{1,0:T(8,128)(2,1)S(1)} %bitcast.20, f32[136,512]{1,0:T(8,128)S(1)} %get-tuple-element.20.gate, bf16[128,128]{1,0:T(8,128)(2,1)S(1)} %copy-done.4), custom_call_target="tpu_custom_call" | custom-call | tf_op jit(solution)/shard_map/pallas_call | solution.py:205
Async XLA Ops:
  39.9 24.1 %copy-start.2 = (bf16[128,512]{1,0:T(8,128)(2,1)S(1)}, bf16[128,512]{1,0:T(8,128)(2,1)}, u32[]{:S(2)}) copy-start(bf16[128,512]{1,0:T(8,128)(2,1)} %get-tuple-element.13.pair) | copy-start | bytes 393220
  40.5 23.6 %copy-start = (f32[136,512]{1,0:T(8,128)S(1)}, f32[136,512]{1,0:T(8,128)}, u32[]{:S(2)}) copy-start(f32[136,512]{1,0:T(8,128)} %get-tuple-element.15.gate) | copy-start | bytes 835588
  40.5 23.6 %copy-start.1 = (bf16[128,640]{1,0:T(8,128)(2,1)S(1)}, bf16[128,640]{1,0:T(8,128)(2,1)}, u32[]{:S(2)}) copy-start(bf16[128,640]{1,0:T(8,128)(2,1)} %weight.1) | copy-start | bytes 491524
  40.5 23.5 %copy-start.3 = (bf16[128,128]{1,0:T(8,128)(2,1)S(1)}, bf16[128,128]{1,0:T(8,128)(2,1)}, u32[]{:S(2)}) copy-start(bf16[128,128]{1,0:T(8,128)(2,1)} %weight_out.2) | copy-start | bytes 98308
  95.7 17.0 %copy-start.4 = (bf16[128,128]{1,0:T(8,128)(2,1)S(1)}, bf16[128,128]{1,0:T(8,128)(2,1)}, u32[]{:S(2)}) copy-start(bf16[128,128]{1,0:T(8,128)(2,1)} %weight_out.3) | copy-start | bytes 98308

commit v6 on v5

--- a/solution.py
+++ b/solution.py
@@ -12,8 +12,9 @@
 
 AXES = ("z2", "z1", "z0", "yb", "ya", "yc", "x1", "x0", "core")
 ROW, COL = AXES[:5], AXES[5:]
-GROUP = ("yc", "yb", "ya", "z0", "z1", "z2", "x0")
-SUM_GROUP = GROUP + ("x1",)
+OUT_GROUP = ("yb", "ya", "z0", "z1", "z2", "x1", "x0")
+SUM_GROUP = OUT_GROUP + ("yc",)
+IN_GROUP = ("yc", "yb", "ya", "z0", "z1", "z2", "x0")
 
 
 NT = (((1,), (1,)), ((), ()))
@@ -55,11 +56,11 @@
     return place
 
 
-def gather_blocks(got):
+def gather_blocks(got, group, col_names):
     values = got[...].astype(F32)
     blocks = []
     for c in range(4):
-        places = [place_in(GROUP, {**bits(ROW, r), **bits(("yc", "x0"), c)}) for r in range(32)]
+        places = [place_in(group, {**bits(ROW, r), **bits(col_names, c)}) for r in range(32)]
         blocks.append(jnp.concatenate([values[8 * p : 8 * (p + 1)] for p in places], axis=0))
     return transpose_groups(blocks)
 
@@ -161,7 +162,7 @@
 
 
 def split_kernel_out(got, both, stage, order):
-    for g, block in enumerate(gather_blocks(got)):
+    for g, block in enumerate(gather_blocks(got, OUT_GROUP, ("x1", "x0"))):
         stage[...] = block
         both[128 * g : 128 * (g + 1), :] = stage[pl.ds(0, 128, stride=2), :].astype(BF16)
         order[pl.ds(g, 128, stride=4), :] = stage[pl.ds(1, 128, stride=2), :]
@@ -184,7 +185,7 @@
 
 
 def split_kernel_in(got, left, right, stage):
-    for g, block in enumerate(gather_blocks(got)):
+    for g, block in enumerate(gather_blocks(got, IN_GROUP, ("yc", "x0"))):
         stage[...] = block
         rows = slice(128 * g, 128 * (g + 1))
         left[:, rows] = stage[pl.ds(0, 128, stride=2), :].T.astype(BF16)
@@ -195,7 +196,7 @@
     stage[...] = dot(left[...], right[...])
     blocks = [stage[pl.ds(g, 128, stride=4), :] for g in range(4)]
     for c, block in enumerate(transpose_groups(blocks)):
-        scatter_block(block, packed, GROUP, ("z1", "yb", "z2", "z0", "ya"), bits(("yc", "x0"), c))
+        scatter_block(block, packed, IN_GROUP, ("z1", "yb", "z2", "z0", "ya"), bits(("yc", "x0"), c))
     sent[...] = packed[...].astype(BF16)
 
 
@@ -231,7 +232,7 @@
         pair, owi, *params,
         hbm=True,
     )
-    got = exchange(sent, GROUP, 8)
+    got = exchange(sent, OUT_GROUP, 8)
     (both,) = call(split_kernel_out, [((1024, 128), BF16)], [(256, 128), (512, 128)], got)
     both = lax.all_gather(both, "core", axis=0, tiled=True)
     (sent,) = call(product_kernel_out, [((1024, 128), BF16)], [(1024, 128)], both)
@@ -242,7 +243,7 @@
         [(1024, 128), (1024, 128)],
         pair, got, gate, owo, iwi,
     )
-    got = exchange(sent, GROUP, 8)
+    got = exchange(sent, IN_GROUP, 8)
     left, right = call(
         split_kernel_in,
         [((128, 512), BF16), ((512, 128), BF16)],
@@ -253,7 +254,7 @@
     (sent,) = call(
         product_kernel_in, [((512, 128), BF16)], [(512, 128), (512, 128)], left, right
     )
-    got = exchange(sent, GROUP, 4)
+    got = exchange(sent, IN_GROUP, 4)
     (updated,) = call(
         close_kernel,
         [((ROWS, COLS, CH), BF16)],

time: 114 us -> 113 us (level)
  no operation moved by 1% of the time
where the time goes in v6:
time: 113 us
  blocking collectives  106 us (94%)
  Pallas kernels  6.74 us (6%)
    all_to_all x4, blocking collectives, exchange(): got = lax.all_to_all(values.reshape(-1, size, 128), group, 0, 0, tiled=True)  89.9 us
    all_gather x1, blocking collectives, shards(): left = lax.all_gather(left, ('x1', 'core'), axis=0, tiled=True)  11.6 us
    pallas_call x7, Pallas kernels, call(): pl.pallas_call(kernel, out_shape=outs, in_specs=[pl.BlockSpec(memory_spac...  6.74 us
    all_gather x1, blocking collectives, shards(): both = lax.all_gather(both, 'core', axis=0, tiled=True)  4.64 us

profile of v6, /device:TPU:1, one launch (start us, length us, event | category | flops | bytes accessed | tf_op | source)
XLA Modules:
  0.0 113.1 jit_solution(7116963128479353790)
XLA Ops:
  0.0 2.7 %shard_map.127 = (bf16[1024,128]{1,0:T(8,128)(2,1)}, f32[136,512]{1,0:T(8,128)}, bf16[128,512]{1,0:T(8,128)(2,1)}) custom-call(bf16[14,28,128]{2,1,0:T(8,128)(2,1)} %refs_0_.1, bf16[128,640]{1,0:T(8,128)(2,1)} %refs_1_.1, f32[1,128]{1,0:T(1,128)} %bitcast.24, f32[1,128]{1,0:T(1,128)} %bitcast.25, f32[1,128]{1,0:T(1,128)} %bitcast.26, f32[1,128]{1,0:T(1,128)} %bitcast.27, ...), custom_call_target="tpu_custom_call" | custom-call | tf_op jit(solution)/shard_map/pallas_call | solution.py:206
  2.7 30.6 %all_to_all.20 = bf16[128,8,128]{2,1,0:T(8,128)(2,1)S(1)} all-to-all(bf16[128,8,128]{2,1,0:T(8,128)(2,1)} %bitcast.23), channel_id=1, replica_groups=mesh['z2'=2,'z1'=2,'z0'=2,'yb'=2,'ya'=2,'yc'=2,'x1'=2,'x0'=2,'core'=2] {..., dimensions={0} | all-to-all | bytes 524288 | tf_op jit(solution)/shard_map/all_to_all | solution.py:217
  33.3 0.3 shard_map.128
  33.6 4.6 %all_gather.6.both = bf16[2048,128]{1,0:T(8,128)(2,1)S(1)} all-gather(bf16[1024,128]{1,0:T(8,128)(2,1)S(1)} %shard_map.128), channel_id=1, replica_groups=mesh['z2'=2,'z1'=2,'z0'=2,'yb'=2,'ya'=2,'yc'=2,'x1'=2,'x0'=2,'core'=2] {..., dimensions={0}, use_global_device_ids=true | all-gather | bytes 786432 | tf_op jit(solution)/shard_map/all_gather | solution.py:237
  38.3 0.0 copy-start.2
  38.3 0.5 shard_map.129
  38.8 0.0 copy-start
  38.8 0.0 copy-start.1
  38.8 0.0 copy-start.3
  38.8 23.2 %all_to_all.21 = bf16[256,4,128]{2,1,0:T(4,128)(2,1)S(1)} all-to-all(bf16[256,4,128]{2,1,0:T(4,128)(2,1)S(1)} %bitcast.16), channel_id=1, replica_groups=mesh['z2'=2,'z1'=2,'z0'=2,'yb'=2,'ya'=2,'yc'=2,'x1'=2,'x0'=2,'core'=2] {..., dimensions={0} | all-to-all | bytes 524288 | tf_op jit(solution)/shard_map/all_to_all | solution.py:217
  62.1 0.0 copy-done.2
  62.1 0.0 copy-done
  62.1 0.0 copy-done.1
  62.1 0.0 copy-done.3
  62.1 1.0 shard_map.130
  63.1 19.1 %all_to_all.22 = bf16[128,8,128]{2,1,0:T(8,128)(2,1)S(1)} all-to-all(bf16[128,8,128]{2,1,0:T(8,128)(2,1)S(1)} %bitcast.22), channel_id=1, replica_groups=mesh['z2'=2,'z1'=2,'z0'=2,'yb'=2,'ya'=2,'yc'=2,'x1'=2,'x0'=2,'core'=2] {..., dimensions={0} | all-to-all | bytes 524288 | tf_op jit(solution)/shard_map/all_to_all | solution.py:217
  82.2 0.4 shard_map.131
  82.6 11.6 %all_gather.7.left = bf16[512,512]{1,0:T(8,128)(2,1)S(1)} all-gather(bf16[128,512]{1,0:T(8,128)(2,1)S(1)} %get-tuple-element.18), channel_id=1, replica_groups=mesh['z2'=2,'z1'=2,'z0'=2,'yb'=2,'ya'=2,'yc'=2,'x1'=2,'x0'=2,'core'=2] {..., dimensions={0}, use_global_device_ids=true | all-gather | bytes 655360 | tf_op jit(solution)/shard_map/all_gather | solution.py:253
  94.2 0.5 shard_map.132
  94.7 0.0 copy-start.4
  94.7 17.0 %all_to_all.23 = bf16[128,4,128]{2,1,0:T(4,128)(2,1)S(1)} all-to-all(bf16[128,4,128]{2,1,0:T(4,128)(2,1)S(1)} %bitcast.21), channel_id=1, replica_groups=mesh['z2'=2,'z1'=2,'z0'=2,'yb'=2,'ya'=2,'yc'=2,'x1'=2,'x0'=2,'core'=2] {..., dimensions={0} | all-to-all | bytes 262144 | tf_op jit(solution)/shard_map/all_to_all | solution.py:217
  111.7 0.0 copy-done.4
  111.7 1.3 %shard_map.133 = bf16[14,28,128]{2,1,0:T(8,128)(2,1)} custom-call(bf16[128,512]{1,0:T(8,128)(2,1)S(1)} %get-tuple-element.16.first, bf16[512,128]{1,0:T(8,128)(2,1)S(1)} %bitcast.20, f32[136,512]{1,0:T(8,128)S(1)} %get-tuple-element.20.gate, bf16[128,128]{1,0:T(8,128)(2,1)S(1)} %copy-done.4), custom_call_target="tpu_custom_call" | custom-call | tf_op jit(solution)/shard_map/pallas_call | solution.py:206
Async XLA Ops:
  38.3 23.8 %copy-start.2 = (bf16[128,512]{1,0:T(8,128)(2,1)S(1)}, bf16[128,512]{1,0:T(8,128)(2,1)}, u32[]{:S(2)}) copy-start(bf16[128,512]{1,0:T(8,128)(2,1)} %get-tuple-element.13.pair) | copy-start | bytes 393220
  38.8 23.3 %copy-start = (f32[136,512]{1,0:T(8,128)S(1)}, f32[136,512]{1,0:T(8,128)}, u32[]{:S(2)}) copy-start(f32[136,512]{1,0:T(8,128)} %get-tuple-element.15.gate) | copy-start | bytes 835588
  38.8 23.3 %copy-start.1 = (bf16[128,640]{1,0:T(8,128)(2,1)S(1)}, bf16[128,640]{1,0:T(8,128)(2,1)}, u32[]{:S(2)}) copy-start(bf16[128,640]{1,0:T(8,128)(2,1)} %weight.1) | copy-start | bytes 491524
  38.8 23.3 %copy-start.3 = (bf16[128,128]{1,0:T(8,128)(2,1)S(1)}, bf16[128,128]{1,0:T(8,128)(2,1)}, u32[]{:S(2)}) copy-start(bf16[128,128]{1,0:T(8,128)(2,1)} %weight_out.2) | copy-start | bytes 98308
  94.7 17.0 %copy-start.4 = (bf16[128,128]{1,0:T(8,128)(2,1)S(1)}, bf16[128,128]{1,0:T(8,128)(2,1)}, u32[]{:S(2)}) copy-start(bf16[128,128]{1,0:T(8,128)(2,1)} %weight_out.3) | copy-start | bytes 98308

commit v7 on v6

--- a/solution.py
+++ b/solution.py
@@ -14,7 +14,7 @@
 ROW, COL = AXES[:5], AXES[5:]
 OUT_GROUP = ("yb", "ya", "z0", "z1", "z2", "x1", "x0")
 SUM_GROUP = OUT_GROUP + ("yc",)
-IN_GROUP = ("yc", "yb", "ya", "z0", "z1", "z2", "x0")
+IN_GROUP = ('yb', 'ya', 'z2', 'z1', 'z0', 'yc', 'x0')
 
 
 NT = (((1,), (1,)), ((), ()))

time: 113 us -> 112 us (level)
  no operation moved by 1% of the time
where the time goes in v7:
time: 112 us
  blocking collectives  105 us (94%)
  Pallas kernels  6.74 us (6%)
    all_to_all x4, blocking collectives, exchange(): got = lax.all_to_all(values.reshape(-1, size, 128), group, 0, 0, tiled=True)  89.3 us
    all_gather x1, blocking collectives, shards(): left = lax.all_gather(left, ('x1', 'core'), axis=0, tiled=True)  11.3 us
    pallas_call x7, Pallas kernels, call(): pl.pallas_call(kernel, out_shape=outs, in_specs=[pl.BlockSpec(memory_spac...  6.74 us
    all_gather x1, blocking collectives, shards(): both = lax.all_gather(both, 'core', axis=0, tiled=True)  4.64 us

profile of v7, /device:TPU:1, one launch (start us, length us, event | category | flops | bytes accessed | tf_op | source)
XLA Modules:
  0.0 112.1 jit_solution(6722789068406182528)
XLA Ops:
  0.0 2.7 %shard_map.127 = (bf16[1024,128]{1,0:T(8,128)(2,1)}, f32[136,512]{1,0:T(8,128)}, bf16[128,512]{1,0:T(8,128)(2,1)}) custom-call(bf16[14,28,128]{2,1,0:T(8,128)(2,1)} %refs_0_.1, bf16[128,640]{1,0:T(8,128)(2,1)} %refs_1_.1, f32[1,128]{1,0:T(1,128)} %bitcast.24, f32[1,128]{1,0:T(1,128)} %bitcast.25, f32[1,128]{1,0:T(1,128)} %bitcast.26, f32[1,128]{1,0:T(1,128)} %bitcast.27, ...), custom_call_target="tpu_custom_call" | custom-call | tf_op jit(solution)/shard_map/pallas_call | solution.py:206
  2.7 30.6 %all_to_all.20 = bf16[128,8,128]{2,1,0:T(8,128)(2,1)S(1)} all-to-all(bf16[128,8,128]{2,1,0:T(8,128)(2,1)} %bitcast.23), channel_id=1, replica_groups=mesh['z2'=2,'z1'=2,'z0'=2,'yb'=2,'ya'=2,'yc'=2,'x1'=2,'x0'=2,'core'=2] {..., dimensions={0} | all-to-all | bytes 524288 | tf_op jit(solution)/shard_map/all_to_all | solution.py:217
  33.3 0.3 shard_map.128
  33.6 4.6 %all_gather.6.both = bf16[2048,128]{1,0:T(8,128)(2,1)S(1)} all-gather(bf16[1024,128]{1,0:T(8,128)(2,1)S(1)} %shard_map.128), channel_id=1, replica_groups=mesh['z2'=2,'z1'=2,'z0'=2,'yb'=2,'ya'=2,'yc'=2,'x1'=2,'x0'=2,'core'=2] {..., dimensions={0}, use_global_device_ids=true | all-gather | bytes 786432 | tf_op jit(solution)/shard_map/all_gather | solution.py:237
  38.3 0.0 copy-start.2
  38.3 0.5 shard_map.129
  38.8 0.0 copy-start
  38.8 0.0 copy-start.1
  38.8 0.0 copy-start.3
  38.8 23.2 %all_to_all.21 = bf16[256,4,128]{2,1,0:T(4,128)(2,1)S(1)} all-to-all(bf16[256,4,128]{2,1,0:T(4,128)(2,1)S(1)} %bitcast.16), channel_id=1, replica_groups=mesh['z2'=2,'z1'=2,'z0'=2,'yb'=2,'ya'=2,'yc'=2,'x1'=2,'x0'=2,'core'=2] {..., dimensions={0} | all-to-all | bytes 524288 | tf_op jit(solution)/shard_map/all_to_all | solution.py:217
  62.1 0.0 copy-done.2
  62.1 0.0 copy-done
  62.1 0.0 copy-done.1
  62.1 0.0 copy-done.3
  62.1 1.0 shard_map.130
  63.1 18.9 %all_to_all.22 = bf16[128,8,128]{2,1,0:T(8,128)(2,1)S(1)} all-to-all(bf16[128,8,128]{2,1,0:T(8,128)(2,1)S(1)} %bitcast.22), channel_id=1, replica_groups=mesh['z2'=2,'z1'=2,'z0'=2,'yb'=2,'ya'=2,'yc'=2,'x1'=2,'x0'=2,'core'=2] {..., dimensions={0} | all-to-all | bytes 524288 | tf_op jit(solution)/shard_map/all_to_all | solution.py:217
  82.0 0.4 shard_map.131
  82.4 11.3 %all_gather.7.left = bf16[512,512]{1,0:T(8,128)(2,1)S(1)} all-gather(bf16[128,512]{1,0:T(8,128)(2,1)S(1)} %get-tuple-element.18), channel_id=1, replica_groups=mesh['z2'=2,'z1'=2,'z0'=2,'yb'=2,'ya'=2,'yc'=2,'x1'=2,'x0'=2,'core'=2] {..., dimensions={0}, use_global_device_ids=true | all-gather | bytes 655360 | tf_op jit(solution)/shard_map/all_gather | solution.py:253
  93.7 0.5 shard_map.132
  94.2 0.0 copy-start.4
  94.2 16.6 %all_to_all.23 = bf16[128,4,128]{2,1,0:T(4,128)(2,1)S(1)} all-to-all(bf16[128,4,128]{2,1,0:T(4,128)(2,1)S(1)} %bitcast.21), channel_id=1, replica_groups=mesh['z2'=2,'z1'=2,'z0'=2,'yb'=2,'ya'=2,'yc'=2,'x1'=2,'x0'=2,'core'=2] {..., dimensions={0} | all-to-all | bytes 262144 | tf_op jit(solution)/shard_map/all_to_all | solution.py:217
  110.8 0.0 copy-done.4
  110.8 1.3 %shard_map.133 = bf16[14,28,128]{2,1,0:T(8,128)(2,1)} custom-call(bf16[128,512]{1,0:T(8,128)(2,1)S(1)} %get-tuple-element.16.first, bf16[512,128]{1,0:T(8,128)(2,1)S(1)} %bitcast.20, f32[136,512]{1,0:T(8,128)S(1)} %get-tuple-element.20.gate, bf16[128,128]{1,0:T(8,128)(2,1)S(1)} %copy-done.4), custom_call_target="tpu_custom_call" | custom-call | tf_op jit(solution)/shard_map/pallas_call | solution.py:206
Async XLA Ops:
  38.3 23.8 %copy-start.2 = (bf16[128,512]{1,0:T(8,128)(2,1)S(1)}, bf16[128,512]{1,0:T(8,128)(2,1)}, u32[]{:S(2)}) copy-start(bf16[128,512]{1,0:T(8,128)(2,1)} %get-tuple-element.13.pair) | copy-start | bytes 393220
  38.8 23.3 %copy-start = (f32[136,512]{1,0:T(8,128)S(1)}, f32[136,512]{1,0:T(8,128)}, u32[]{:S(2)}) copy-start(f32[136,512]{1,0:T(8,128)} %get-tuple-element.15.gate) | copy-start | bytes 835588
  38.8 23.3 %copy-start.1 = (bf16[128,640]{1,0:T(8,128)(2,1)S(1)}, bf16[128,640]{1,0:T(8,128)(2,1)}, u32[]{:S(2)}) copy-start(bf16[128,640]{1,0:T(8,128)(2,1)} %weight.1) | copy-start | bytes 491524
  38.8 23.3 %copy-start.3 = (bf16[128,128]{1,0:T(8,128)(2,1)S(1)}, bf16[128,128]{1,0:T(8,128)(2,1)}, u32[]{:S(2)}) copy-start(bf16[128,128]{1,0:T(8,128)(2,1)} %weight_out.2) | copy-start | bytes 98308
  94.2 16.6 %copy-start.4 = (bf16[128,128]{1,0:T(8,128)(2,1)S(1)}, bf16[128,128]{1,0:T(8,128)(2,1)}, u32[]{:S(2)}) copy-start(bf16[128,128]{1,0:T(8,128)(2,1)} %weight_out.3) | copy-start | bytes 98308

commit v8 on v7

--- a/solution.py
+++ b/solution.py
@@ -14,7 +14,7 @@
 ROW, COL = AXES[:5], AXES[5:]
 OUT_GROUP = ("yb", "ya", "z0", "z1", "z2", "x1", "x0")
 SUM_GROUP = OUT_GROUP + ("yc",)
-IN_GROUP = ('yb', 'ya', 'z2', 'z1', 'z0', 'yc', 'x0')
+IN_GROUP = ("yb", "ya", "z2", "z1", "z0", "x0", "yc")
 
 
 NT = (((1,), (1,)), ((), ()))

time: 112 us -> 112 us (level)
  no operation moved by 1% of the time
where the time goes in v8:
time: 112 us
  blocking collectives  105 us (94%)
  Pallas kernels  6.73 us (6%)
    all_to_all x4, blocking collectives, exchange(): got = lax.all_to_all(values.reshape(-1, size, 128), group, 0, 0, tiled=True)  89.3 us
    all_gather x1, blocking collectives, shards(): left = lax.all_gather(left, ('x1', 'core'), axis=0, tiled=True)  11.3 us
    pallas_call x7, Pallas kernels, call(): pl.pallas_call(kernel, out_shape=outs, in_specs=[pl.BlockSpec(memory_spac...  6.73 us
    all_gather x1, blocking collectives, shards(): both = lax.all_gather(both, 'core', axis=0, tiled=True)  4.64 us

profile of v8, /device:TPU:1, one launch (start us, length us, event | category | flops | bytes accessed | tf_op | source)
XLA Modules:
  0.0 112.1 jit_solution(6217280726616773934)
XLA Ops:
  0.0 2.7 %shard_map.127 = (bf16[1024,128]{1,0:T(8,128)(2,1)}, f32[136,512]{1,0:T(8,128)}, bf16[128,512]{1,0:T(8,128)(2,1)}) custom-call(bf16[14,28,128]{2,1,0:T(8,128)(2,1)} %refs_0_.1, bf16[128,640]{1,0:T(8,128)(2,1)} %refs_1_.1, f32[1,128]{1,0:T(1,128)} %bitcast.24, f32[1,128]{1,0:T(1,128)} %bitcast.25, f32[1,128]{1,0:T(1,128)} %bitcast.26, f32[1,128]{1,0:T(1,128)} %bitcast.27, ...), custom_call_target="tpu_custom_call" | custom-call | tf_op jit(solution)/shard_map/pallas_call | solution.py:206
  2.7 30.6 %all_to_all.20 = bf16[128,8,128]{2,1,0:T(8,128)(2,1)S(1)} all-to-all(bf16[128,8,128]{2,1,0:T(8,128)(2,1)} %bitcast.23), channel_id=1, replica_groups=mesh['z2'=2,'z1'=2,'z0'=2,'yb'=2,'ya'=2,'yc'=2,'x1'=2,'x0'=2,'core'=2] {..., dimensions={0} | all-to-all | bytes 524288 | tf_op jit(solution)/shard_map/all_to_all | solution.py:217
  33.3 0.3 shard_map.128
  33.6 4.6 %all_gather.6.both = bf16[2048,128]{1,0:T(8,128)(2,1)S(1)} all-gather(bf16[1024,128]{1,0:T(8,128)(2,1)S(1)} %shard_map.128), channel_id=1, replica_groups=mesh['z2'=2,'z1'=2,'z0'=2,'yb'=2,'ya'=2,'yc'=2,'x1'=2,'x0'=2,'core'=2] {..., dimensions={0}, use_global_device_ids=true | all-gather | bytes 786432 | tf_op jit(solution)/shard_map/all_gather | solution.py:237
  38.3 0.0 copy-start.2
  38.3 0.5 shard_map.129
  38.8 0.0 copy-start
  38.8 0.0 copy-start.1
  38.8 0.0 copy-start.3
  38.8 23.2 %all_to_all.21 = bf16[256,4,128]{2,1,0:T(4,128)(2,1)S(1)} all-to-all(bf16[256,4,128]{2,1,0:T(4,128)(2,1)S(1)} %bitcast.16), channel_id=1, replica_groups=mesh['z2'=2,'z1'=2,'z0'=2,'yb'=2,'ya'=2,'yc'=2,'x1'=2,'x0'=2,'core'=2] {..., dimensions={0} | all-to-all | bytes 524288 | tf_op jit(solution)/shard_map/all_to_all | solution.py:217
  62.1 0.0 copy-done.2
  62.1 0.0 copy-done
  62.1 0.0 copy-done.1
  62.1 0.0 copy-done.3
  62.1 1.0 shard_map.130
  63.1 18.8 %all_to_all.22 = bf16[128,8,128]{2,1,0:T(8,128)(2,1)S(1)} all-to-all(bf16[128,8,128]{2,1,0:T(8,128)(2,1)S(1)} %bitcast.22), channel_id=1, replica_groups=mesh['z2'=2,'z1'=2,'z0'=2,'yb'=2,'ya'=2,'yc'=2,'x1'=2,'x0'=2,'core'=2] {..., dimensions={0} | all-to-all | bytes 524288 | tf_op jit(solution)/shard_map/all_to_all | solution.py:217
  81.9 0.4 shard_map.131
  82.3 11.3 %all_gather.7.left = bf16[512,512]{1,0:T(8,128)(2,1)S(1)} all-gather(bf16[128,512]{1,0:T(8,128)(2,1)S(1)} %get-tuple-element.18), channel_id=1, replica_groups=mesh['z2'=2,'z1'=2,'z0'=2,'yb'=2,'ya'=2,'yc'=2,'x1'=2,'x0'=2,'core'=2] {..., dimensions={0}, use_global_device_ids=true | all-gather | bytes 655360 | tf_op jit(solution)/shard_map/all_gather | solution.py:253
  93.6 0.5 shard_map.132
  94.1 0.0 copy-start.4
  94.1 16.6 %all_to_all.23 = bf16[128,4,128]{2,1,0:T(4,128)(2,1)S(1)} all-to-all(bf16[128,4,128]{2,1,0:T(4,128)(2,1)S(1)} %bitcast.21), channel_id=1, replica_groups=mesh['z2'=2,'z1'=2,'z0'=2,'yb'=2,'ya'=2,'yc'=2,'x1'=2,'x0'=2,'core'=2] {..., dimensions={0} | all-to-all | bytes 262144 | tf_op jit(solution)/shard_map/all_to_all | solution.py:217
  110.7 0.0 copy-done.4
  110.7 1.3 %shard_map.133 = bf16[14,28,128]{2,1,0:T(8,128)(2,1)} custom-call(bf16[128,512]{1,0:T(8,128)(2,1)S(1)} %get-tuple-element.16.first, bf16[512,128]{1,0:T(8,128)(2,1)S(1)} %bitcast.20, f32[136,512]{1,0:T(8,128)S(1)} %get-tuple-element.20.gate, bf16[128,128]{1,0:T(8,128)(2,1)S(1)} %copy-done.4), custom_call_target="tpu_custom_call" | custom-call | tf_op jit(solution)/shard_map/pallas_call | solution.py:206
Async XLA Ops:
  38.3 23.8 %copy-start.2 = (bf16[128,512]{1,0:T(8,128)(2,1)S(1)}, bf16[128,512]{1,0:T(8,128)(2,1)}, u32[]{:S(2)}) copy-start(bf16[128,512]{1,0:T(8,128)(2,1)} %get-tuple-element.13.pair) | copy-start | bytes 393220
  38.8 23.3 %copy-start = (f32[136,512]{1,0:T(8,128)S(1)}, f32[136,512]{1,0:T(8,128)}, u32[]{:S(2)}) copy-start(f32[136,512]{1,0:T(8,128)} %get-tuple-element.15.gate) | copy-start | bytes 835588
  38.8 23.3 %copy-start.1 = (bf16[128,640]{1,0:T(8,128)(2,1)S(1)}, bf16[128,640]{1,0:T(8,128)(2,1)}, u32[]{:S(2)}) copy-start(bf16[128,640]{1,0:T(8,128)(2,1)} %weight.1) | copy-start | bytes 491524
  38.8 23.3 %copy-start.3 = (bf16[128,128]{1,0:T(8,128)(2,1)S(1)}, bf16[128,128]{1,0:T(8,128)(2,1)}, u32[]{:S(2)}) copy-start(bf16[128,128]{1,0:T(8,128)(2,1)} %weight_out.2) | copy-start | bytes 98308
  94.1 16.7 %copy-start.4 = (bf16[128,128]{1,0:T(8,128)(2,1)S(1)}, bf16[128,128]{1,0:T(8,128)(2,1)}, u32[]{:S(2)}) copy-start(bf16[128,128]{1,0:T(8,128)(2,1)} %weight_out.3) | copy-start | bytes 98308

commit v9 on v7

--- a/solution.py
+++ b/solution.py
@@ -196,7 +196,7 @@
     stage[...] = dot(left[...], right[...])
     blocks = [stage[pl.ds(g, 128, stride=4), :] for g in range(4)]
     for c, block in enumerate(transpose_groups(blocks)):
-        scatter_block(block, packed, IN_GROUP, ("z1", "yb", "z2", "z0", "ya"), bits(("yc", "x0"), c))
+        scatter_block(block, packed, IN_GROUP, ("yb", "z1", "z2", "z0", "ya"), bits(("yc", "x0"), c))
     sent[...] = packed[...].astype(BF16)
 
 
@@ -250,7 +250,7 @@
         [(256, 128)],
         got,
     )
-    left = lax.all_gather(left, ("x1", "core"), axis=0, tiled=True)
+    left = lax.all_gather(left, ("core", "x1"), axis=0, tiled=True)
     (sent,) = call(
         product_kernel_in, [((512, 128), BF16)], [(512, 128), (512, 128)], left, right
     )

time: 112 us -> 120 us (1.071)
  blocking collectives: 105 us -> 112 us
    all_gather x1, blocking collectives: 11.3 us -> 18.5 us  [shards(): left = lax.all_gather(left, ('core', 'x1'), axis=0, tiled=True)]
where the time goes in v9:
time: 120 us; the launch traced here: 119 us
  blocking collectives  112 us (93%)
  Pallas kernels  6.75 us (6%)
    all_to_all x4, blocking collectives, exchange(): got = lax.all_to_all(values.reshape(-1, size, 128), group, 0, 0, tiled=True)  89 us
    all_gather x1, blocking collectives, shards(): left = lax.all_gather(left, ('core', 'x1'), axis=0, tiled=True)  18.5 us
    pallas_call x7, Pallas kernels, call(): pl.pallas_call(kernel, out_shape=outs, in_specs=[pl.BlockSpec(memory_spac...  6.75 us
    all_gather x1, blocking collectives, shards(): both = lax.all_gather(both, 'core', axis=0, tiled=True)  4.64 us

profile of v9, /device:TPU:1, one launch (start us, length us, event | category | flops | bytes accessed | tf_op | source)
XLA Modules:
  0.0 119.0 jit_solution(11554592516235604356)
XLA Ops:
  0.0 2.7 %shard_map.127 = (bf16[1024,128]{1,0:T(8,128)(2,1)}, f32[136,512]{1,0:T(8,128)}, bf16[128,512]{1,0:T(8,128)(2,1)}) custom-call(bf16[14,28,128]{2,1,0:T(8,128)(2,1)} %refs_0_.1, bf16[128,640]{1,0:T(8,128)(2,1)} %refs_1_.1, f32[1,128]{1,0:T(1,128)} %bitcast.24, f32[1,128]{1,0:T(1,128)} %bitcast.25, f32[1,128]{1,0:T(1,128)} %bitcast.26, f32[1,128]{1,0:T(1,128)} %bitcast.27, ...), custom_call_target="tpu_custom_call" | custom-call | tf_op jit(solution)/shard_map/pallas_call | solution.py:206
  2.7 30.6 %all_to_all.20 = bf16[128,8,128]{2,1,0:T(8,128)(2,1)S(1)} all-to-all(bf16[128,8,128]{2,1,0:T(8,128)(2,1)} %bitcast.23), channel_id=1, replica_groups=mesh['z2'=2,'z1'=2,'z0'=2,'yb'=2,'ya'=2,'yc'=2,'x1'=2,'x0'=2,'core'=2] {..., dimensions={0} | all-to-all | bytes 524288 | tf_op jit(solution)/shard_map/all_to_all | solution.py:217
  33.3 0.3 shard_map.128
  33.6 4.6 %all_gather.6.both = bf16[2048,128]{1,0:T(8,128)(2,1)S(1)} all-gather(bf16[1024,128]{1,0:T(8,128)(2,1)S(1)} %shard_map.128), channel_id=1, replica_groups=mesh['z2'=2,'z1'=2,'z0'=2,'yb'=2,'ya'=2,'yc'=2,'x1'=2,'x0'=2,'core'=2] {..., dimensions={0}, use_global_device_ids=true | all-gather | bytes 786432 | tf_op jit(solution)/shard_map/all_gather | solution.py:237
  38.3 0.0 copy-start.2
  38.3 0.5 shard_map.129
  38.8 0.0 copy-start
  38.8 0.0 copy-start.1
  38.8 0.0 copy-start.3
  38.8 23.2 %all_to_all.21 = bf16[256,4,128]{2,1,0:T(4,128)(2,1)S(1)} all-to-all(bf16[256,4,128]{2,1,0:T(4,128)(2,1)S(1)} %bitcast.16), channel_id=1, replica_groups=mesh['z2'=2,'z1'=2,'z0'=2,'yb'=2,'ya'=2,'yc'=2,'x1'=2,'x0'=2,'core'=2] {..., dimensions={0} | all-to-all | bytes 524288 | tf_op jit(solution)/shard_map/all_to_all | solution.py:217
  62.1 0.0 copy-done.2
  62.1 0.0 copy-done
  62.1 0.0 copy-done.1
  62.1 0.0 copy-done.3
  62.1 1.0 shard_map.130
  63.1 18.9 %all_to_all.22 = bf16[128,8,128]{2,1,0:T(8,128)(2,1)S(1)} all-to-all(bf16[128,8,128]{2,1,0:T(8,128)(2,1)S(1)} %bitcast.22), channel_id=1, replica_groups=mesh['z2'=2,'z1'=2,'z0'=2,'yb'=2,'ya'=2,'yc'=2,'x1'=2,'x0'=2,'core'=2] {..., dimensions={0} | all-to-all | bytes 524288 | tf_op jit(solution)/shard_map/all_to_all | solution.py:217
  82.0 0.4 shard_map.131
  82.4 18.5 %all_gather.7.left = bf16[512,512]{1,0:T(8,128)(2,1)S(1)} all-gather(bf16[128,512]{1,0:T(8,128)(2,1)S(1)} %get-tuple-element.18), channel_id=1, replica_groups=mesh['z2'=2,'z1'=2,'z0'=2,'yb'=2,'ya'=2,'yc'=2,'x1'=2,'x0'=2,'core'=2] {..., dimensions={0}, use_global_device_ids=true | all-gather | bytes 655360 | tf_op jit(solution)/shard_map/all_gather | solution.py:253
  100.8 0.5 shard_map.132
  101.3 0.0 copy-start.4
  101.3 16.3 %all_to_all.23 = bf16[128,4,128]{2,1,0:T(4,128)(2,1)S(1)} all-to-all(bf16[128,4,128]{2,1,0:T(4,128)(2,1)S(1)} %bitcast.21), channel_id=1, replica_groups=mesh['z2'=2,'z1'=2,'z0'=2,'yb'=2,'ya'=2,'yc'=2,'x1'=2,'x0'=2,'core'=2] {..., dimensions={0} | all-to-all | bytes 262144 | tf_op jit(solution)/shard_map/all_to_all | solution.py:217
  117.7 0.0 copy-done.4
  117.7 1.3 %shard_map.133 = bf16[14,28,128]{2,1,0:T(8,128)(2,1)} custom-call(bf16[128,512]{1,0:T(8,128)(2,1)S(1)} %get-tuple-element.16.first, bf16[512,128]{1,0:T(8,128)(2,1)S(1)} %bitcast.20, f32[136,512]{1,0:T(8,128)S(1)} %get-tuple-element.20.gate, bf16[128,128]{1,0:T(8,128)(2,1)S(1)} %copy-done.4), custom_call_target="tpu_custom_call" | custom-call | tf_op jit(solution)/shard_map/pallas_call | solution.py:206
Async XLA Ops:
  38.3 23.8 %copy-start.2 = (bf16[128,512]{1,0:T(8,128)(2,1)S(1)}, bf16[128,512]{1,0:T(8,128)(2,1)}, u32[]{:S(2)}) copy-start(bf16[128,512]{1,0:T(8,128)(2,1)} %get-tuple-element.13.pair) | copy-start | bytes 393220
  38.8 23.3 %copy-start = (f32[136,512]{1,0:T(8,128)S(1)}, f32[136,512]{1,0:T(8,128)}, u32[]{:S(2)}) copy-start(f32[136,512]{1,0:T(8,128)} %get-tuple-element.15.gate) | copy-start | bytes 835588
  38.8 23.3 %copy-start.1 = (bf16[128,640]{1,0:T(8,128)(2,1)S(1)}, bf16[128,640]{1,0:T(8,128)(2,1)}, u32[]{:S(2)}) copy-start(bf16[128,640]{1,0:T(8,128)(2,1)} %weight.1) | copy-start | bytes 491524
  38.8 23.3 %copy-start.3 = (bf16[128,128]{1,0:T(8,128)(2,1)S(1)}, bf16[128,128]{1,0:T(8,128)(2,1)}, u32[]{:S(2)}) copy-start(bf16[128,128]{1,0:T(8,128)(2,1)} %weight_out.2) | copy-start | bytes 98308
  101.3 16.3 %copy-start.4 = (bf16[128,128]{1,0:T(8,128)(2,1)S(1)}, bf16[128,128]{1,0:T(8,128)(2,1)}, u32[]{:S(2)}) copy-start(bf16[128,128]{1,0:T(8,128)(2,1)} %weight_out.3) | copy-start | bytes 98308
